TPU v7x, 768 devices: a whole 4x8x12 slice. The times are simulated.
768 devices in a mesh: group: 96 (over z, x, core), head: 8 (over y).
Axes of the slice: x: 4, y: 8, z: 12, core: 2. Of those that a mesh axis runs over, the one named last changes fastest.
Arguments:
- query: bfloat16 [49152, 1792], P('group', 'head'), may hold values from -6 to 6
- key_in: bfloat16 [49152, 1792], P('group', 'head'), may hold values from -6 to 6
- value: bfloat16 [49152, 1792], P('group', 'head'), may hold values from -6 to 6
- proj: bfloat16 [1792, 2240], P('head'), may hold values from -0.125 to 0.125
- cot: bfloat16 [2240, 49152], P('head', 'group'), may hold values from -6 to 6
- lengths: int32 [96], replicated, may hold values from 128 to 512, as said below
Outputs:
- mixed: bfloat16 [2240, 49152], P('head', 'group')
- query_gradient: bfloat16 [49152, 1792], P('group', 'head')
- key_gradient: bfloat16 [49152, 1792], P('group', 'head')
- value_gradient: bfloat16 [49152, 1792], P('group', 'head')
Inputs may be any that keep to these rules, and one draw needn't show every extreme that they name: `lengths`: every entry is a multiple of 128, and some block holds exactly 512 live tokens in every draw.
All inputs are finite; a program needn't handle non-finite values.
Results may differ from a plain program's by a relative error of at most 0.0067.
Values may be sent and summed in bfloat16 or wider, within the bound.
No kernel may reach another device: no remote copies, remote signals or barrier semaphores. Data moves between devices by JAX's collectives and lax.ppermute only.
A program may use at most 32 MiB of HBM per device.

v0:
```python
import jax
import jax.numpy as jnp
from jax import lax
from jax.sharding import PartitionSpec as P

HEAD_DIM = 112


def passed_along(block, axis, distance):
    devices = range(lax.axis_size(axis))
    route = [(i - distance, i) for i in devices if i - distance in devices]
    return lax.ppermute(block, axis, route)


def pack_pair(square, vector):
    return jnp.concatenate([square, vector[:, None, :]], axis=1)


def earlier_sums(square, vector):
    count = lax.axis_size("group")
    own = pack_pair(square, vector)
    running = own
    distance = 1
    while distance < count:
        running = running + passed_along(running, "group", distance)
        distance = distance * 2
    before = running - own
    return (before[:, :-1, :], before[:, -1, :])


def later_sums(square, vector):
    count = lax.axis_size("group")
    own = pack_pair(square, vector)
    running = own
    distance = 1
    while distance < count:
        running = running + passed_along(running, "group", -distance)
        distance = distance * 2
    after = running - own
    return (after[:, :-1, :], after[:, -1, :])


def block_scores(feat_q, key_features, values, pair):
    scores = jnp.einsum("thd,shd->hts", feat_q, key_features, preferred_element_type=jnp.float32)
    masked = jnp.where(pair[None], scores, 0.0)
    weights = masked.astype(jnp.bfloat16)
    local_num = jnp.einsum("hts,shd->thd", weights, values, preferred_element_type=jnp.float32)
    local_den = jnp.sum(masked, axis=2).T
    return (weights, local_num, local_den)


def per_device(query, key_in, value, proj, cot, lengths):
    high = lax.Precision.HIGHEST
    capacity_limit = query.shape[0]
    block_width = query.shape[1]
    heads = block_width // HEAD_DIM
    position = lax.axis_index("group")
    live = lengths[position]
    slots = jnp.arange(capacity_limit, dtype=jnp.int32)
    valid_tokens = slots < live
    pair = (slots[:, None] >= slots[None, :]) & valid_tokens[:, None] & valid_tokens[None, :]
    valid_mask = valid_tokens[:, None, None]
    unactivated_query = query.reshape(capacity_limit, heads, HEAD_DIM)
    unactivated_key = key_in.reshape(capacity_limit, heads, HEAD_DIM)
    feat_q = jax.nn.relu(unactivated_query)
    key_features = jax.nn.relu(unactivated_key)
    values = value.reshape(capacity_limit, heads, HEAD_DIM)
    masked_key_rows = jnp.where(valid_mask, key_features, jnp.zeros_like(key_features))
    state_loc = jnp.einsum(
        "shd,she->hde", masked_key_rows, values, preferred_element_type=jnp.float32
    )
    ksum_loc = jnp.sum(masked_key_rows.astype(jnp.float32), axis=0)
    state_prev, ksum_prev = earlier_sums(state_loc, ksum_loc)
    weights, local_num, local_den = block_scores(feat_q, key_features, values, pair)
    query_f = feat_q.astype(jnp.float32)
    numerator = local_num + jnp.einsum("thd,hde->the", query_f, state_prev, precision=high)
    denominator = local_den + jnp.einsum("thd,hd->th", query_f, ksum_prev, precision=high) + 1.0
    attention_block = jnp.where(valid_mask, numerator / denominator[:, :, None], 0.0).astype(
        jnp.bfloat16
    )
    attn_flat = attention_block.reshape(capacity_limit, block_width)
    mixed = lax.psum_scatter(
        lax.dot_general(
            proj, attn_flat, (((0,), (1,)), ((), ())), preferred_element_type=jnp.float32
        ),
        "head",
        scatter_dimension=0,
        tiled=True,
    ).astype(jnp.bfloat16)
    grad_sum = lax.dot_general(
        lax.all_gather(cot, "head", axis=0, tiled=True),
        proj,
        (((0,), (1,)), ((), ())),
        preferred_element_type=jnp.float32,
    )
    grad_attn = lax.optimization_barrier(grad_sum.astype(jnp.bfloat16)).astype(jnp.float32)
    head_gradients = grad_attn.reshape(capacity_limit, heads, HEAD_DIM)
    numerator_gradient = jnp.where(valid_mask, head_gradients / denominator[:, :, None], 0.0)
    d_den = jnp.where(
        valid_tokens[:, None],
        -jnp.sum(head_gradients * numerator, axis=2) / (denominator * denominator),
        0.0,
    )
    d_num_b = numerator_gradient.astype(jnp.bfloat16)
    adj_loc = jnp.einsum("thd,the->hde", feat_q, d_num_b, preferred_element_type=jnp.float32)
    adj_sum_loc = jnp.einsum("th,thd->hd", d_den, query_f, precision=high)
    adj_next, adj_sum_next = later_sums(adj_loc, adj_sum_loc)
    d_scores = (
        jnp.einsum("the,she->hts", d_num_b, values, preferred_element_type=jnp.float32)
        + d_den.T[:, :, None]
    )
    d_scores = jnp.where(pair[None], d_scores, 0.0).astype(jnp.bfloat16)
    query_feature_gradient = jnp.einsum(
        "hts,shd->thd", d_scores, key_features, preferred_element_type=jnp.float32
    )
    query_feature_gradient = (
        query_feature_gradient
        + jnp.einsum("the,hde->thd", numerator_gradient, state_prev, precision=high)
        + d_den[:, :, None] * ksum_prev[None]
    )
    key_feature_gradient = jnp.einsum(
        "hts,thd->shd", d_scores, feat_q, preferred_element_type=jnp.float32
    )
    key_feature_gradient = (
        key_feature_gradient
        + jnp.einsum("she,hde->shd", values.astype(jnp.float32), adj_next, precision=high)
        + adj_sum_next[None]
    )
    value_gradient_local = jnp.einsum(
        "hts,the->she", weights, d_num_b, preferred_element_type=jnp.float32
    )
    value_gradient_local = value_gradient_local + jnp.einsum(
        "shd,hde->she", key_features.astype(jnp.float32), adj_next, precision=high
    )
    query_gradient = (
        jnp.where(valid_mask & (unactivated_query > 0), query_feature_gradient, 0.0)
        .astype(jnp.bfloat16)
        .reshape(capacity_limit, block_width)
    )
    key_gradient = (
        jnp.where(valid_mask & (unactivated_key > 0), key_feature_gradient, 0.0)
        .astype(jnp.bfloat16)
        .reshape(capacity_limit, block_width)
    )
    value_gradient = (
        jnp.where(valid_mask, value_gradient_local, 0.0)
        .astype(jnp.bfloat16)
        .reshape(capacity_limit, block_width)
    )
    return (mixed, query_gradient, key_gradient, value_gradient)


def solution(mesh):
    return jax.shard_map(
        per_device,
        mesh=mesh,
        in_specs=(
            P("group", "head"),
            P("group", "head"),
            P("group", "head"),
            P("head", None),
            P("head", "group"),
            P(),
        ),
        out_specs=(P("head", "group"), P("group", "head"), P("group", "head"), P("group", "head")),
        check_vma=False,
    )
```

profile of v0, /device:TPU:222, one launch (start us, length us, event | category | flops | bytes accessed | tf_op | source)
XLA Modules:
  0.0 177.6 jit_solution(18329978034893435516)
XLA Ops:
  15.3 4.2 %collective-permute-done = f32[2,113,112]{1,2,0:T(8,128)S(1)} collective-permute-done((f32[2,113,112]{1,2,0:T(8,128)S(1)}, f32[2,113,112]{1,2,0:T(8,128)S(1)}, u32[]{:S(2)}, u32[]{:S(2)}) %collective-permute-start) | collective-permute-done | bytes 101280 | tf_op jit(solution)/shard_map/ppermute | solution.py:12
  19.6 8.7 %collective-permute-start.1 = (f32[2,113,112]{1,2,0:T(8,128)S(1)}, f32[2,113,112]{1,2,0:T(8,128)S(1)}, u32[]{:S(2)}, u32[]{:S(2)}) collective-permute-start(f32[2,113,112]{1,2,0:T(8,128)S(1)} %fusion.67), channel_id=1, source_target_pairs={{0,16},{8,24},{16,32},{24,40},{32,48},{40,56},{48,64},{56,72},{64,... | collective-permute-start | bytes 303752 | tf_op jit(solution)/shard_map/ppermute | solution.py:12
  28.3 2.3 %collective-permute-done.1 = f32[2,113,112]{1,2,0:T(8,128)S(1)} collective-permute-done((f32[2,113,112]{1,2,0:T(8,128)S(1)}, f32[2,113,112]{1,2,0:T(8,128)S(1)}, u32[]{:S(2)}, u32[]{:S(2)}) %collective-permute-start.1) | collective-permute-done | bytes 101280 | tf_op jit(solution)/shard_map/ppermute | solution.py:12
  30.7 3.8 %collective-permute-start.2 = (f32[2,113,112]{1,2,0:T(8,128)S(1)}, f32[2,113,112]{1,2,0:T(8,128)S(1)}, u32[]{:S(2)}, u32[]{:S(2)}) collective-permute-start(f32[2,113,112]{1,2,0:T(8,128)S(1)} %add.105), channel_id=1, source_target_pairs={{0,32},{8,40},{16,48},{24,56},{32,64},{40,72},{48,80},{56,88},{64,... | collective-permute-start | bytes 303752 | tf_op jit(solution)/shard_map/ppermute | solution.py:12
  34.5 4.4 %collective-permute-done.2 = f32[2,113,112]{1,2,0:T(8,128)S(1)} collective-permute-done((f32[2,113,112]{1,2,0:T(8,128)S(1)}, f32[2,113,112]{1,2,0:T(8,128)S(1)}, u32[]{:S(2)}, u32[]{:S(2)}) %collective-permute-start.2) | collective-permute-done | bytes 101280 | tf_op jit(solution)/shard_map/ppermute | solution.py:12
  38.9 3.2 %collective-permute-start.3 = (f32[2,113,112]{1,2,0:T(8,128)S(1)}, f32[2,113,112]{1,2,0:T(8,128)S(1)}, u32[]{:S(2)}, u32[]{:S(2)}) collective-permute-start(f32[2,113,112]{1,2,0:T(8,128)S(1)} %add.106), channel_id=1, source_target_pairs={{0,64},{8,72},{16,80},{24,88},{32,96},{40,104},{48,112},{56,120},{... | collective-permute-start | bytes 303752 | tf_op jit(solution)/shard_map/ppermute | solution.py:12
  42.2 3.6 %collective-permute-done.3 = f32[2,113,112]{1,2,0:T(8,128)S(1)} collective-permute-done((f32[2,113,112]{1,2,0:T(8,128)S(1)}, f32[2,113,112]{1,2,0:T(8,128)S(1)}, u32[]{:S(2)}, u32[]{:S(2)}) %collective-permute-start.3) | collective-permute-done | bytes 101280 | tf_op jit(solution)/shard_map/ppermute | solution.py:12
  45.8 4.9 %collective-permute-start.4 = (f32[2,113,112]{1,2,0:T(8,128)S(1)}, f32[2,113,112]{1,2,0:T(8,128)S(1)}, u32[]{:S(2)}, u32[]{:S(2)}) collective-permute-start(f32[2,113,112]{1,2,0:T(8,128)S(1)} %add.107), channel_id=1, source_target_pairs={{0,128},{8,136},{16,144},{24,152},{32,160},{40,168},{48,176},{56,1... | collective-permute-start | bytes 303752 | tf_op jit(solution)/shard_map/ppermute | solution.py:12
  50.8 3.4 %collective-permute-done.4 = f32[2,113,112]{1,2,0:T(8,128)S(1)} collective-permute-done((f32[2,113,112]{1,2,0:T(8,128)S(1)}, f32[2,113,112]{1,2,0:T(8,128)S(1)}, u32[]{:S(2)}, u32[]{:S(2)}) %collective-permute-start.4) | collective-permute-done | bytes 101280 | tf_op jit(solution)/shard_map/ppermute | solution.py:12
  54.2 8.7 %collective-permute-start.5 = (f32[2,113,112]{1,2,0:T(8,128)S(1)}, f32[2,113,112]{1,2,0:T(8,128)S(1)}, u32[]{:S(2)}, u32[]{:S(2)}) collective-permute-start(f32[2,113,112]{1,2,0:T(8,128)S(1)} %add.108), channel_id=1, source_target_pairs={{0,256},{8,264},{16,272},{24,280},{32,288},{40,296},{48,304},{56,3... | collective-permute-start | bytes 303752 | tf_op jit(solution)/shard_map/ppermute | solution.py:12
  63.5 4.6 %collective-permute-done.5 = f32[2,113,112]{1,2,0:T(8,128)S(1)} collective-permute-done((f32[2,113,112]{1,2,0:T(8,128)S(1)}, f32[2,113,112]{1,2,0:T(8,128)S(1)}, u32[]{:S(2)}, u32[]{:S(2)}) %collective-permute-start.5) | collective-permute-done | bytes 101280 | tf_op jit(solution)/shard_map/ppermute | solution.py:12
  68.2 3.3 %collective-permute-start.6 = (f32[2,113,112]{1,2,0:T(8,128)S(1)}, f32[2,113,112]{1,2,0:T(8,128)S(1)}, u32[]{:S(2)}, u32[]{:S(2)}) collective-permute-start(f32[2,113,112]{1,2,0:T(8,128)S(1)} %add.109), channel_id=1, source_target_pairs={{0,512},{8,520},{16,528},{24,536},{32,544},{40,552},{48,560},{56,5... | collective-permute-start | bytes 303752 | tf_op jit(solution)/shard_map/ppermute | solution.py:12
  74.3 2.3 %convolution_convert_fusion = bf16[512,224]{0,1:T(8,128)(2,1)S(1)} fusion(bf16[224,2240]{1,0:T(8,128)(2,1)S(1)} %copy-done, bf16[2240,512]{1,0:T(8,128)(2,1)} %all-gather.2.cloned.1.call-done), kind=kOutput, calls=%fused_computation.20 | convolution fusion | flops 513916928 | bytes 3526656 | tf_op jit(solution)/shard_map/dot_general | solution.py:90
  77.1 2.9 %convolution_bitcast_fusion = f32[2240,512]{1,0:T(8,128)} fusion(bf16[512,224]{0,1:T(8,128)(2,1)S(1)} %bitcast.97, bf16[224,2240]{1,0:T(8,128)(2,1)S(1)} %copy-done), kind=kOutput, calls=%fused_computation | convolution fusion | flops 513802240 | bytes 5820416 | tf_op jit(solution)/shard_map/dot_general | solution.py:83
  82.8 2.3 %collective-permute-done.7 = f32[2,113,112]{1,2,0:T(8,128)S(1)} collective-permute-done((f32[2,113,112]{1,2,0:T(8,128)S(1)}, f32[2,113,112]{1,2,0:T(8,128)S(1)}, u32[]{:S(2)}, u32[]{:S(2)}) %collective-permute-start.7) | collective-permute-done | bytes 101280 | tf_op jit(solution)/shard_map/ppermute | solution.py:12
  85.2 6.2 %collective-permute-start.8 = (f32[2,113,112]{1,2,0:T(8,128)S(1)}, f32[2,113,112]{1,2,0:T(8,128)S(1)}, u32[]{:S(2)}, u32[]{:S(2)}) collective-permute-start(f32[2,113,112]{1,2,0:T(8,128)S(1)} %fusion.66), channel_id=1, source_target_pairs={{16,0},{24,8},{32,16},{40,24},{48,32},{56,40},{64,48},{72,56},{80,... | collective-permute-start | bytes 303752 | tf_op jit(solution)/shard_map/ppermute | solution.py:12
  91.9 7.6 %collective-permute-done.8 = f32[2,113,112]{1,2,0:T(8,128)S(1)} collective-permute-done((f32[2,113,112]{1,2,0:T(8,128)S(1)}, f32[2,113,112]{1,2,0:T(8,128)S(1)}, u32[]{:S(2)}, u32[]{:S(2)}) %collective-permute-start.8) | collective-permute-done | bytes 101280 | tf_op jit(solution)/shard_map/ppermute | solution.py:12
  99.4 2.5 %collective-permute-start.9 = (f32[2,113,112]{1,2,0:T(8,128)S(1)}, f32[2,113,112]{1,2,0:T(8,128)S(1)}, u32[]{:S(2)}, u32[]{:S(2)}) collective-permute-start(f32[2,113,112]{1,2,0:T(8,128)S(1)} %add.122), channel_id=1, source_target_pairs={{32,0},{40,8},{48,16},{56,24},{64,32},{72,40},{80,48},{88,56},{96,... | collective-permute-start | bytes 303752 | tf_op jit(solution)/shard_map/ppermute | solution.py:12
  102.0 7.7 %collective-permute-done.9 = f32[2,113,112]{1,2,0:T(8,128)S(1)} collective-permute-done((f32[2,113,112]{1,2,0:T(8,128)S(1)}, f32[2,113,112]{1,2,0:T(8,128)S(1)}, u32[]{:S(2)}, u32[]{:S(2)}) %collective-permute-start.9) | collective-permute-done | bytes 101280 | tf_op jit(solution)/shard_map/ppermute | solution.py:12
  112.3 5.4 %collective-permute-done.10 = f32[2,113,112]{1,2,0:T(8,128)S(1)} collective-permute-done((f32[2,113,112]{1,2,0:T(8,128)S(1)}, f32[2,113,112]{1,2,0:T(8,128)S(1)}, u32[]{:S(2)}, u32[]{:S(2)}) %collective-permute-start.10) | collective-permute-done | bytes 101280 | tf_op jit(solution)/shard_map/ppermute | solution.py:12
  117.7 5.2 %collective-permute-start.11 = (f32[2,113,112]{1,2,0:T(8,128)S(1)}, f32[2,113,112]{1,2,0:T(8,128)S(1)}, u32[]{:S(2)}, u32[]{:S(2)}) collective-permute-start(f32[2,113,112]{1,2,0:T(8,128)S(1)} %add.124), channel_id=1, source_target_pairs={{128,0},{136,8},{144,16},{152,24},{160,32},{168,40},{176,48},{184,... | collective-permute-start | bytes 303752 | tf_op jit(solution)/shard_map/ppermute | solution.py:12
  123.3 3.6 %collective-permute-done.11 = f32[2,113,112]{1,2,0:T(8,128)S(1)} collective-permute-done((f32[2,113,112]{1,2,0:T(8,128)S(1)}, f32[2,113,112]{1,2,0:T(8,128)S(1)}, u32[]{:S(2)}, u32[]{:S(2)}) %collective-permute-start.11) | collective-permute-done | bytes 101280 | tf_op jit(solution)/shard_map/ppermute | solution.py:12
  128.6 24.5 %collective-permute-done.12 = f32[2,113,112]{1,2,0:T(8,128)S(1)} collective-permute-done((f32[2,113,112]{1,2,0:T(8,128)S(1)}, f32[2,113,112]{1,2,0:T(8,128)S(1)}, u32[]{:S(2)}, u32[]{:S(2)}) %collective-permute-start.12) | collective-permute-done | bytes 101280 | tf_op jit(solution)/shard_map/ppermute | solution.py:12
  155.7 10.8 %collective-permute-done.13 = f32[2,113,112]{1,2,0:T(8,128)S(1)} collective-permute-done((f32[2,113,112]{1,2,0:T(8,128)S(1)}, f32[2,113,112]{1,2,0:T(8,128)S(1)}, u32[]{:S(2)}, u32[]{:S(2)}) %collective-permute-start.13) | collective-permute-done | bytes 101280 | tf_op jit(solution)/shard_map/ppermute | solution.py:12
  (69 shorter events, 27.1 us)
Async XLA Ops:
  7.2 67.2 %copy-start = (bf16[224,2240]{1,0:T(8,128)(2,1)S(1)}, bf16[224,2240]{1,0:T(8,128)(2,1)}, u32[]{:S(2)}) copy-start(bf16[224,2240]{1,0:T(8,128)(2,1)} %param.9) | copy-start | bytes 3010564
  7.2 35.0 %copy-start.2 = (bf16[512,224]{0,1:T(8,128)(2,1)S(1)}, bf16[512,224]{0,1:T(8,128)(2,1)}, u32[]{:S(2)}) copy-start(bf16[512,224]{0,1:T(8,128)(2,1)} %param.6) | copy-start | bytes 688132
  7.2 67.1 %all-gather.2.cloned.1.call-start = ((), (), s32[]{:S(2)}) async-start(), calls=%async_computation.2 | async-start | bytes 2580480 | tf_op jit(solution)/shard_map/all_gather | solution.py:91
  7.9 161.0 %reduce-scatter.2.cloned.1.call-start = ((), (), s32[]{:S(2)}) async-start(), calls=%async_computation.1 | async-start | bytes 5160960 | tf_op jit(solution)/shard_map/reduce_scatter | solution.py:82
  13.4 6.1 %collective-permute-start = (f32[2,113,112]{1,2,0:T(8,128)S(1)}, f32[2,113,112]{1,2,0:T(8,128)S(1)}, u32[]{:S(2)}, u32[]{:S(2)}) collective-permute-start(f32[2,113,112]{1,2,0:T(8,128)S(1)} %pad_maximum_fusion), channel_id=1, source_target_pairs={{0,8},{8,16},{16,24},{24,32},{32,40},{40,48},{48,56},{56,64},{64,7... | collective-permute-start | bytes 303752 | tf_op jit(solution)/shard_map/ppermute | solution.py:12
  19.6 11.1 %collective-permute-start.1 = (f32[2,113,112]{1,2,0:T(8,128)S(1)}, f32[2,113,112]{1,2,0:T(8,128)S(1)}, u32[]{:S(2)}, u32[]{:S(2)}) collective-permute-start(f32[2,113,112]{1,2,0:T(8,128)S(1)} %fusion.67), channel_id=1, source_target_pairs={{0,16},{8,24},{16,32},{24,40},{32,48},{40,56},{48,64},{56,72},{64,... | collective-permute-start | bytes 303752 | tf_op jit(solution)/shard_map/ppermute | solution.py:12
  30.7 8.2 %collective-permute-start.2 = (f32[2,113,112]{1,2,0:T(8,128)S(1)}, f32[2,113,112]{1,2,0:T(8,128)S(1)}, u32[]{:S(2)}, u32[]{:S(2)}) collective-permute-start(f32[2,113,112]{1,2,0:T(8,128)S(1)} %add.105), channel_id=1, source_target_pairs={{0,32},{8,40},{16,48},{24,56},{32,64},{40,72},{48,80},{56,88},{64,... | collective-permute-start | bytes 303752 | tf_op jit(solution)/shard_map/ppermute | solution.py:12
  38.9 32.5 %copy-start.3 = (bf16[512,224]{0,1:T(8,128)(2,1)S(1)}, bf16[512,224]{0,1:T(8,128)(2,1)}, u32[]{:S(2)}) copy-start(bf16[512,224]{0,1:T(8,128)(2,1)} %param.8) | copy-start | bytes 688132
  38.9 6.8 %collective-permute-start.3 = (f32[2,113,112]{1,2,0:T(8,128)S(1)}, f32[2,113,112]{1,2,0:T(8,128)S(1)}, u32[]{:S(2)}, u32[]{:S(2)}) collective-permute-start(f32[2,113,112]{1,2,0:T(8,128)S(1)} %add.106), channel_id=1, source_target_pairs={{0,64},{8,72},{16,80},{24,88},{32,96},{40,104},{48,112},{56,120},{... | collective-permute-start | bytes 303752 | tf_op jit(solution)/shard_map/ppermute | solution.py:12
  45.8 8.4 %collective-permute-start.4 = (f32[2,113,112]{1,2,0:T(8,128)S(1)}, f32[2,113,112]{1,2,0:T(8,128)S(1)}, u32[]{:S(2)}, u32[]{:S(2)}) collective-permute-start(f32[2,113,112]{1,2,0:T(8,128)S(1)} %add.107), channel_id=1, source_target_pairs={{0,128},{8,136},{16,144},{24,152},{32,160},{40,168},{48,176},{56,1... | collective-permute-start | bytes 303752 | tf_op jit(solution)/shard_map/ppermute | solution.py:12
  54.2 13.9 %collective-permute-start.5 = (f32[2,113,112]{1,2,0:T(8,128)S(1)}, f32[2,113,112]{1,2,0:T(8,128)S(1)}, u32[]{:S(2)}, u32[]{:S(2)}) collective-permute-start(f32[2,113,112]{1,2,0:T(8,128)S(1)} %add.108), channel_id=1, source_target_pairs={{0,256},{8,264},{16,272},{24,280},{32,288},{40,296},{48,304},{56,3... | collective-permute-start | bytes 303752 | tf_op jit(solution)/shard_map/ppermute | solution.py:12
  63.5 10.8 %copy-start.4 = (bf16[2,512,512]{1,2,0:T(8,128)(2,1)}, bf16[2,512,512]{1,2,0:T(8,128)(2,1)S(1)}, u32[]{:S(2)}) copy-start(bf16[2,512,512]{1,2,0:T(8,128)(2,1)S(1)} %get-tuple-element.7) | copy-start | bytes 3145732
  68.2 5.6 %collective-permute-start.6 = (f32[2,113,112]{1,2,0:T(8,128)S(1)}, f32[2,113,112]{1,2,0:T(8,128)S(1)}, u32[]{:S(2)}, u32[]{:S(2)}) collective-permute-start(f32[2,113,112]{1,2,0:T(8,128)S(1)} %add.109), channel_id=1, source_target_pairs={{0,512},{8,520},{16,528},{24,536},{32,544},{40,552},{48,560},{56,5... | collective-permute-start | bytes 303752 | tf_op jit(solution)/shard_map/ppermute | solution.py:12
  80.1 2.7 %copy-start.1 = (bf16[512,224]{0,1:T(8,128)(2,1)S(1)}, bf16[512,224]{0,1:T(8,128)(2,1)}, u32[]{:S(2)}) copy-start(bf16[512,224]{0,1:T(8,128)(2,1)} %param.7) | copy-start | bytes 688132
  80.1 11.3 %copy-start.5 = (bf16[2,512,512]{1,2,0:T(8,128)(2,1)S(1)}, bf16[2,512,512]{1,2,0:T(8,128)(2,1)}, u32[]{:S(2)}) copy-start(bf16[2,512,512]{1,2,0:T(8,128)(2,1)} %copy-done.4) | copy-start | bytes 3145732
  80.8 4.3 %collective-permute-start.7 = (f32[2,113,112]{1,2,0:T(8,128)S(1)}, f32[2,113,112]{1,2,0:T(8,128)S(1)}, u32[]{:S(2)}, u32[]{:S(2)}) collective-permute-start(f32[2,113,112]{1,2,0:T(8,128)S(1)} %pad_maximum_fusion.1), channel_id=1, source_target_pairs={{8,0},{16,8},{24,16},{32,24},{40,32},{48,40},{56,48},{64,56},{72,6... | collective-permute-start | bytes 303752 | tf_op jit(solution)/shard_map/ppermute | solution.py:12
  85.2 14.2 %collective-permute-start.8 = (f32[2,113,112]{1,2,0:T(8,128)S(1)}, f32[2,113,112]{1,2,0:T(8,128)S(1)}, u32[]{:S(2)}, u32[]{:S(2)}) collective-permute-start(f32[2,113,112]{1,2,0:T(8,128)S(1)} %fusion.66), channel_id=1, source_target_pairs={{16,0},{24,8},{32,16},{40,24},{48,32},{56,40},{64,48},{72,56},{80,... | collective-permute-start | bytes 303752 | tf_op jit(solution)/shard_map/ppermute | solution.py:12
  99.4 10.3 %collective-permute-start.9 = (f32[2,113,112]{1,2,0:T(8,128)S(1)}, f32[2,113,112]{1,2,0:T(8,128)S(1)}, u32[]{:S(2)}, u32[]{:S(2)}) collective-permute-start(f32[2,113,112]{1,2,0:T(8,128)S(1)} %add.122), channel_id=1, source_target_pairs={{32,0},{40,8},{48,16},{56,24},{64,32},{72,40},{80,48},{88,56},{96,... | collective-permute-start | bytes 303752 | tf_op jit(solution)/shard_map/ppermute | solution.py:12
  109.8 7.9 %collective-permute-start.10 = (f32[2,113,112]{1,2,0:T(8,128)S(1)}, f32[2,113,112]{1,2,0:T(8,128)S(1)}, u32[]{:S(2)}, u32[]{:S(2)}) collective-permute-start(f32[2,113,112]{1,2,0:T(8,128)S(1)} %add.123), channel_id=1, source_target_pairs={{64,0},{72,8},{80,16},{88,24},{96,32},{104,40},{112,48},{120,56},{... | collective-permute-start | bytes 303752 | tf_op jit(solution)/shard_map/ppermute | solution.py:12
  117.7 9.3 %collective-permute-start.11 = (f32[2,113,112]{1,2,0:T(8,128)S(1)}, f32[2,113,112]{1,2,0:T(8,128)S(1)}, u32[]{:S(2)}, u32[]{:S(2)}) collective-permute-start(f32[2,113,112]{1,2,0:T(8,128)S(1)} %add.124), channel_id=1, source_target_pairs={{128,0},{136,8},{144,16},{152,24},{160,32},{168,40},{176,48},{184,... | collective-permute-start | bytes 303752 | tf_op jit(solution)/shard_map/ppermute | solution.py:12
  127.0 26.1 %collective-permute-start.12 = (f32[2,113,112]{1,2,0:T(8,128)S(1)}, f32[2,113,112]{1,2,0:T(8,128)S(1)}, u32[]{:S(2)}, u32[]{:S(2)}) collective-permute-start(f32[2,113,112]{1,2,0:T(8,128)S(1)} %add.125), channel_id=1, source_target_pairs={{256,0},{264,8},{272,16},{280,24},{288,32},{296,40},{304,48},{312,... | collective-permute-start | bytes 303752 | tf_op jit(solution)/shard_map/ppermute | solution.py:12
  153.1 13.4 %collective-permute-start.13 = (f32[2,113,112]{1,2,0:T(8,128)S(1)}, f32[2,113,112]{1,2,0:T(8,128)S(1)}, u32[]{:S(2)}, u32[]{:S(2)}) collective-permute-start(f32[2,113,112]{1,2,0:T(8,128)S(1)} %add.126), channel_id=1, source_target_pairs={{512,0},{520,8},{528,16},{536,24},{544,32},{552,40},{560,48},{568,... | collective-permute-start | bytes 303752 | tf_op jit(solution)/shard_map/ppermute | solution.py:12
Sparse Core Ops, SparseCore 0:
  10.4 50.2 all-gather.1
  80.2 79.4 reduce-scatter.1
where the time goes:
time: 178 us
  waiting for transfers between devices  87 us (49%)
  starting transfers between devices  54.8 us (31%)
  between operations  14.5 us (8%)
  matrix products  13.9 us (8%)
  other arithmetic  5.58 us (3%)
  local copies, waits for them, and re-layouts  1.83 us (1%)
    ppermute x14, waiting for transfers between devices, passed_along(): return lax.ppermute(block, axis, route)  86.3 us
    ppermute x14, starting transfers between devices, passed_along(): return lax.ppermute(block, axis, route)  54.8 us
  transfers between devices with their start and end apart: 16, of which 14 were waited for; matrix products, arithmetic and copies ran while one was open for 8% of the time, Pallas kernels for 0%

commit v1 on v0

v1 whole, which is shorter than its diff:
```python
import jax
import jax.numpy as jnp
from jax import lax
from jax.sharding import Mesh
from jax.sharding import PartitionSpec as P

HEAD_DIM = 112
PLANE = ("x", "c")
ROWS = 32


def shifted(block, distance):
    count = lax.axis_size("z")
    route = [(i - distance, i) for i in range(count) if 0 <= i - distance < count]
    return lax.ppermute(block, "z", route)


def sums_beyond(packed, sign):
    mine = lax.all_to_all(packed, PLANE, 0, 0)
    inner = mine if sign > 0 else mine[::-1]
    before = [jnp.zeros_like(inner[0])]
    for i in range(inner.shape[0]):
        before.append(before[-1] + inner[i])
    total = before.pop()
    near = shifted(total, sign) + shifted(total, 2 * sign) + shifted(total, 3 * sign)
    window = total + near
    base = near + shifted(window, 4 * sign) + shifted(window, 8 * sign)
    back = jnp.stack(before if sign > 0 else before[::-1]) + base[None]
    return lax.all_to_all(back, PLANE, 0, 0)


def pack(square, vector):
    heads = square.shape[0]
    flat = square.reshape(heads * HEAD_DIM, HEAD_DIM)
    rest = 8 * ROWS - flat.shape[0] - heads
    return jnp.concatenate(
        [flat, vector, jnp.zeros((rest, HEAD_DIM), jnp.float32)], axis=0
    ).reshape(8, ROWS, HEAD_DIM)


def unpack(packed, heads):
    flat = packed.reshape(8 * ROWS, HEAD_DIM)
    n = heads * HEAD_DIM
    return flat[:n].reshape(heads, HEAD_DIM, HEAD_DIM), flat[n : n + heads]


def halves(x):
    top = x.astype(jnp.bfloat16)
    return top, (x - top.astype(jnp.float32)).astype(jnp.bfloat16)


def dot2(spec, left, right):
    top, low = halves(right)
    return jnp.einsum(spec, left, top, preferred_element_type=jnp.float32) + jnp.einsum(
        spec, left, low, preferred_element_type=jnp.float32
    )


def per_device(query, key_in, value, proj, cot, lengths):
    bf, f32 = jnp.bfloat16, jnp.float32
    cap, width = query.shape
    heads = width // HEAD_DIM
    cot_all = lax.all_gather(cot, "y", axis=0, tiled=True)
    live = lengths[lax.axis_index(("z", "x", "c"))]
    slots = jnp.arange(cap, dtype=jnp.int32)
    valid = slots < live
    pair = (slots[:, None] >= slots[None, :]) & valid[:, None] & valid[None, :]
    vmask = valid[:, None, None]
    q3 = query.reshape(cap, heads, HEAD_DIM)
    k3 = key_in.reshape(cap, heads, HEAD_DIM)
    fq = jax.nn.relu(q3)
    fk = jax.nn.relu(k3)
    v3 = value.reshape(cap, heads, HEAD_DIM)
    fk_live = jnp.where(vmask, fk, jnp.zeros_like(fk))
    state_loc = jnp.einsum("shd,she->hde", fk_live, v3, preferred_element_type=f32)
    ksum_loc = jnp.sum(fk_live.astype(f32), axis=0)
    state_prev, ksum_prev = unpack(sums_beyond(pack(state_loc, ksum_loc), 1), heads)

    scores = jnp.einsum("thd,shd->hts", fq, fk, preferred_element_type=f32)
    masked = jnp.where(pair[None], scores, 0.0)
    weights = masked.astype(bf)
    fqf = fq.astype(f32)
    numer = jnp.einsum("hts,shd->thd", weights, v3, preferred_element_type=f32)
    numer = numer + dot2("thd,hde->the", fq, state_prev)
    denom = jnp.sum(masked, axis=2).T + jnp.sum(fqf * ksum_prev[None], axis=2) + 1.0
    inv = 1.0 / denom
    attn = jnp.where(vmask, numer * inv[:, :, None], 0.0).astype(bf).reshape(cap, width)
    terms = lax.dot_general(proj, attn, (((0,), (1,)), ((), ())), preferred_element_type=f32).astype(bf)
    cot_all, terms = lax.optimization_barrier((cot_all, terms))
    mixed = lax.psum_scatter(terms, "y", scatter_dimension=0, tiled=True)

    grad = lax.dot_general(cot_all, proj, (((0,), (1,)), ((), ())), preferred_element_type=f32)
    grad = grad.astype(bf).astype(f32).reshape(cap, heads, HEAD_DIM)
    d_num = jnp.where(vmask, grad * inv[:, :, None], 0.0)
    d_den = jnp.where(valid[:, None], -jnp.sum(grad * numer, axis=2) * inv * inv, 0.0)
    d_num_b = d_num.astype(bf)
    adj_loc = jnp.einsum("thd,the->hde", fq, d_num_b, preferred_element_type=f32)
    adj_sum_loc = jnp.sum(d_den[:, :, None] * fqf, axis=0)
    adj_next, adj_sum_next = unpack(sums_beyond(pack(adj_loc, adj_sum_loc), -1), heads)

    d_scores = jnp.einsum("the,she->hts", d_num_b, v3, preferred_element_type=f32) + d_den.T[:, :, None]
    d_scores = jnp.where(pair[None], d_scores, 0.0).astype(bf)
    gq = jnp.einsum("hts,shd->thd", d_scores, fk, preferred_element_type=f32)
    gq = gq + dot2("the,hde->thd", d_num_b, state_prev) + d_den[:, :, None] * ksum_prev[None]
    gk = jnp.einsum("hts,thd->shd", d_scores, fq, preferred_element_type=f32)
    gk = gk + dot2("she,hde->shd", v3, adj_next) + adj_sum_next[None]
    gv = jnp.einsum("hts,the->she", weights, d_num_b, preferred_element_type=f32)
    gv = gv + dot2("shd,hde->she", fk, adj_next)
    out_q = jnp.where(vmask & (q3 > 0), gq, 0.0).astype(bf).reshape(cap, width)
    out_k = jnp.where(vmask & (k3 > 0), gk, 0.0).astype(bf).reshape(cap, width)
    out_v = jnp.where(vmask, gv, 0.0).astype(bf).reshape(cap, width)
    return mixed, out_q, out_k, out_v


def solution(mesh):
    group, head = mesh.devices.shape
    fine = Mesh(mesh.devices.reshape(group // 8, 4, 2, head), ("z", "x", "c", "y"))
    tokens = ("z", "x", "c")
    return jax.shard_map(
        per_device,
        mesh=fine,
        in_specs=(P(tokens, "y"), P(tokens, "y"), P(tokens, "y"), P("y", None), P("y", tokens), P()),
        out_specs=(P("y", tokens), P(tokens, "y"), P(tokens, "y"), P(tokens, "y")),
        check_vma=False,
    )
```

time: 178 us -> 143 us (0.80)
  the two profiles are of different devices: /device:TPU:222 before, /device:TPU:4 now
where the time goes in v1:
time: 143 us; the launch traced here: 142 us
  starting transfers between devices  59.1 us (41%)
  waiting for transfers between devices  41.5 us (29%)
  matrix products  16.5 us (12%)
  between operations  14.6 us (10%)
  other arithmetic  7.63 us (5%)
  local copies, waits for them, and re-layouts  2.49 us (2%)
    ppermute x10, starting transfers between devices, shifted(): return lax.ppermute(block, 'z', route)  29.6 us
    ppermute x10, waiting for transfers between devices, shifted(): return lax.ppermute(block, 'z', route)  22 us
    all_to_all x2, starting transfers between devices, sums_beyond(): mine = lax.all_to_all(packed, PLANE, 0, 0)  17.6 us
    all_to_all x2, starting transfers between devices, sums_beyond(): return lax.all_to_all(back, PLANE, 0, 0)  11.9 us
    reduce_scatter x1, waiting for transfers between devices, per_device(): mixed = lax.psum_scatter(terms, 'y', scatter_dimension=0, tiled=True)  7.74 us
    all_gather x1, waiting for transfers between devices, per_device(): cot_all = lax.all_gather(cot, 'y', axis=0, tiled=True)  5.29 us
    all_to_all x2, waiting for transfers between devices, sums_beyond(): return lax.all_to_all(back, PLANE, 0, 0)  4.26 us
  transfers between devices with their start and end apart: 16, of which 13 were waited for; matrix products, arithmetic and copies ran while one was open for 11% of the time, Pallas kernels for 0%

profile of v1, /device:TPU:4, one launch (start us, length us, event | category | flops | bytes accessed | tf_op | source)
XLA Modules:
  0.0 141.7 jit_solution(888049581264359958)
XLA Ops:
  13.4 12.8 %all-to-all-start = ((f32[8,32,112]{2,1,0:T(8,128)}), f32[8,32,112]{2,1,0:T(8,128)S(1)}, u32[]{:S(2)}, u32[]{:S(2)}) async-start(f32[8,32,112]{2,1,0:T(8,128)} %bitcast.6), calls=%async_computation | async-start | bytes 262144 | tf_op jit(solution)/shard_map/all_to_all | solution.py:19
  27.1 1.6 %select_reduce_fusion = (f32[2,512]{1,0:T(2,128)S(1)}, bf16[2,512,512]{1,2,0:T(8,128)(2,1)}) fusion(pred[512,512]{0,1:T(8,128)(4,1)S(1)} %fusion.14, bf16[512,2,112]{0,2,1:T(8,128)(2,1)S(1)} %bitcast.87, bf16[512,2,112]{0,2,1:T(8,128)(2,1)S(1)} %bitcast.94), kind=kOutput, calls=%fused_computation.3 | convolution fusion | flops 119012352 | bytes 1773568 | tf_op jit(solution)/shard_map/thd,shd->hts/dot_general | solution.py:79
  29.6 1.4 %collective-permute-start = (f32[32,112]{1,0:T(8,128)S(1)}, f32[32,112]{1,0:T(8,128)S(1)}, u32[]{:S(2)}, u32[]{:S(2)}) collective-permute-start(f32[32,112]{1,0:T(8,128)S(1)} %get-tuple-element.11), channel_id=1, source_target_pairs={{0,64},{64,128},{128,192},{192,256},{256,320},{320,384},{384,448},... | collective-permute-start | bytes 43016 | tf_op jit(solution)/shard_map/ppermute | solution.py:15
  32.4 8.9 %collective-permute-start.2 = (f32[32,112]{1,0:T(8,128)S(1)}, f32[32,112]{1,0:T(8,128)S(1)}, u32[]{:S(2)}, u32[]{:S(2)}) collective-permute-start(f32[32,112]{1,0:T(8,128)S(1)} %get-tuple-element.11), channel_id=1, source_target_pairs={{0,192},{64,256},{128,320},{192,384},{256,448},{320,512},{384,576}... | collective-permute-start | bytes 43016 | tf_op jit(solution)/shard_map/ppermute | solution.py:15
  41.3 1.4 collective-permute-done.2
  42.7 8.7 %collective-permute-start.3 = (f32[32,112]{1,0:T(8,128)S(1)}, f32[32,112]{1,0:T(8,128)S(1)}, u32[]{:S(2)}, u32[]{:S(2)}) collective-permute-start(f32[32,112]{1,0:T(8,128)S(1)} %fusion.49), channel_id=1, source_target_pairs={{0,256},{64,320},{128,384},{192,448},{256,512},{320,576},{384,640}... | collective-permute-start | bytes 43016 | tf_op jit(solution)/shard_map/ppermute | solution.py:15
  51.4 2.8 %collective-permute-start.4 = (f32[32,112]{1,0:T(8,128)S(1)}, f32[32,112]{1,0:T(8,128)S(1)}, u32[]{:S(2)}, u32[]{:S(2)}) collective-permute-start(f32[32,112]{1,0:T(8,128)S(1)} %fusion.49), channel_id=1, source_target_pairs={{0,512},{64,576},{128,640},{192,704},{1,513},{65,577},{129,641},{1... | collective-permute-start | bytes 43016 | tf_op jit(solution)/shard_map/ppermute | solution.py:15
  54.3 1.4 collective-permute-done.4
  56.4 5.8 %all-to-all-start.1 = ((f32[8,32,112]{2,1,0:T(8,128)}), f32[8,32,112]{2,1,0:T(8,128)S(1)}, u32[]{:S(2)}, u32[]{:S(2)}) async-start(f32[8,32,112]{2,1,0:T(8,128)} %broadcast_add_fusion.1), calls=%async_computation.1 | async-start | bytes 262144 | tf_op jit(solution)/shard_map/all_to_all | solution.py:29
  62.9 2.7 %all-to-all-done.1 = f32[8,32,112]{2,1,0:T(8,128)S(1)} async-done(((f32[8,32,112]{2,1,0:T(8,128)}), f32[8,32,112]{2,1,0:T(8,128)S(1)}, u32[]{:S(2)}, u32[]{:S(2)}) %all-to-all-start.1) | async-done | bytes 114720 | tf_op jit(solution)/shard_map/all_to_all | solution.py:29
  67.4 2.2 %fusion = bf16[2240,512]{1,0:T(8,128)(2,1)} fusion(bf16[512,224]{0,1:T(8,128)(2,1)S(1)} %bitcast.114, bf16[224,2240]{1,0:T(8,128)(2,1)S(1)} %copy-done), kind=kOutput, calls=%fused_computation.1 | convolution fusion | flops 514949120 | bytes 3526656 | tf_op jit(solution)/shard_map/dot_general | solution.py:88
  69.6 5.3 %all-gather.2.cloned.1.call-done = bf16[2240,512]{1,0:T(8,128)(2,1)} async-done(((bf16[280,512]{1,0:T(8,128)(2,1)}), bf16[2240,512]{1,0:T(8,128)(2,1)}) %all-gather.2.cloned.1.call-update) | async-done | bytes 2293776 | tf_op jit(solution)/shard_map/all_gather | solution.py:63
  74.9 2.3 %convolution_convert_fusion.1 = bf16[512,224]{0,1:T(8,128)(2,1)S(1)} fusion(bf16[224,2240]{1,0:T(8,128)(2,1)S(1)} %copy-done, bf16[2240,512]{1,0:T(8,128)(2,1)} %all-gather.2.cloned.1.call-done), kind=kOutput, calls=%fused_computation.25 | convolution fusion | flops 513916928 | bytes 3526656 | tf_op jit(solution)/shard_map/dot_general | solution.py:92
  78.7 4.8 %all-to-all-start.2 = ((f32[8,32,112]{2,1,0:T(8,128)}), f32[8,32,112]{2,1,0:T(8,128)S(1)}, u32[]{:S(2)}, u32[]{:S(2)}) async-start(f32[8,32,112]{2,1,0:T(8,128)} %bitcast.24), calls=%async_computation.3 | async-start | bytes 262144 | tf_op jit(solution)/shard_map/all_to_all | solution.py:19
  83.5 1.5 %select_convert_fusion = bf16[2,512,512]{1,2,0:T(8,128)(2,1)S(1)} fusion(bf16[512,2,112]{0,2,1:T(8,128)(2,1)S(1)} %bitcast.112, f32[2,512]{1,0:T(2,128)S(1)} %broadcast_select_fusion, pred[512,512]{0,1:T(8,128)(4,1)} %copy-done.6, bf16[512,2,112]{0,2,1:T(8,128)(2,1)S(1)} %bitcast.104, f32[512,2]{0,1:T(2,128)S(1)} %fusion.27, ...), kind=kOutput, calls=%fused_computation.2 | convolution fusion | flops 119472128 | bytes 1778176 | tf_op jit(solution)/shard_map/the,she->hts/dot_general | solution.py:101
  90.9 1.6 %collective-permute-done.5 = f32[32,112]{1,0:T(8,128)S(1)} collective-permute-done((f32[32,112]{1,0:T(8,128)S(1)}, f32[32,112]{1,0:T(8,128)S(1)}, u32[]{:S(2)}, u32[]{:S(2)}) %collective-permute-start.5) | collective-permute-done | bytes 14368 | tf_op jit(solution)/shard_map/ppermute | solution.py:15
  92.5 3.2 %collective-permute-done.6 = f32[32,112]{1,0:T(8,128)S(1)} collective-permute-done((f32[32,112]{1,0:T(8,128)S(1)}, f32[32,112]{1,0:T(8,128)S(1)}, u32[]{:S(2)}, u32[]{:S(2)}) %collective-permute-start.6) | collective-permute-done | bytes 14368 | tf_op jit(solution)/shard_map/ppermute | solution.py:15
  95.7 3.0 %collective-permute-done.7 = f32[32,112]{1,0:T(8,128)S(1)} collective-permute-done((f32[32,112]{1,0:T(8,128)S(1)}, f32[32,112]{1,0:T(8,128)S(1)}, u32[]{:S(2)}, u32[]{:S(2)}) %collective-permute-start.7) | collective-permute-done | bytes 14368 | tf_op jit(solution)/shard_map/ppermute | solution.py:15
  101.3 7.3 %collective-permute-done.8 = f32[32,112]{1,0:T(8,128)S(1)} collective-permute-done((f32[32,112]{1,0:T(8,128)S(1)}, f32[32,112]{1,0:T(8,128)S(1)}, u32[]{:S(2)}, u32[]{:S(2)}) %collective-permute-start.8) | collective-permute-done | bytes 14368 | tf_op jit(solution)/shard_map/ppermute | solution.py:15
  108.6 4.1 %collective-permute-done.9 = f32[32,112]{1,0:T(8,128)S(1)} collective-permute-done((f32[32,112]{1,0:T(8,128)S(1)}, f32[32,112]{1,0:T(8,128)S(1)}, u32[]{:S(2)}, u32[]{:S(2)}) %collective-permute-start.9) | collective-permute-done | bytes 14368 | tf_op jit(solution)/shard_map/ppermute | solution.py:15
  113.4 6.0 %all-to-all-start.3 = ((f32[8,32,112]{2,1,0:T(8,128)}), f32[8,32,112]{2,1,0:T(8,128)S(1)}, u32[]{:S(2)}, u32[]{:S(2)}) async-start(f32[8,32,112]{2,1,0:T(8,128)} %broadcast_add_fusion), calls=%async_computation.4 | async-start | bytes 262144 | tf_op jit(solution)/shard_map/all_to_all | solution.py:29
  119.4 1.9 %fusion.12 = bf16[512,2,112]{0,2,1:T(8,128)(2,1)} fusion(f32[2,112,512]{2,1,0:T(8,128)S(1)} %convolution_add_fusion.5, bf16[512,2,112]{0,2,1:T(8,128)(2,1)S(1)} %bitcast.95, bf16[2,512,512]{1,2,0:T(8,128)(2,1)S(1)} %select_convert_fusion, pred[512,2,112]{0,2,1:T(8,128)(4,1)} %bitcast.119, f32[512,2]{0,1:T(2,128)S(1)} %fusion.24, f32[2,112]{1,0:T(2,128)S(1)} %slice.99, ...), kind=kOutput, calls=%fused_computation.24 | convolution fusion | flops 118128640 | bytes 2086272 | tf_op jit(solution)/shard_map/hts,shd->thd/dot_general | solution.py:103
  121.3 1.5 %all-to-all-done.3 = f32[8,32,112]{2,1,0:T(8,128)S(1)} async-done(((f32[8,32,112]{2,1,0:T(8,128)}), f32[8,32,112]{2,1,0:T(8,128)S(1)}, u32[]{:S(2)}, u32[]{:S(2)}) %all-to-all-start.3) | async-done | bytes 114720 | tf_op jit(solution)/shard_map/all_to_all | solution.py:29
  127.1 7.7 %reduce-scatter.2.cloned.1.call-done = bf16[280,512]{1,0:T(8,128)(2,1)} async-done(((bf16[2240,512]{1,0:T(8,128)(2,1)}), bf16[280,512]{1,0:T(8,128)(2,1)}) %reduce-scatter.2.cloned.1.call-update) | async-done | bytes 286736 | tf_op jit(solution)/shard_map/reduce_scatter | solution.py:90
  (97 shorter events, 27.0 us)
Async XLA Ops:
  7.2 60.2 %copy-start = (bf16[224,2240]{1,0:T(8,128)(2,1)S(1)}, bf16[224,2240]{1,0:T(8,128)(2,1)}, u32[]{:S(2)}) copy-start(bf16[224,2240]{1,0:T(8,128)(2,1)} %param.9) | copy-start | bytes 3010564
  7.2 19.9 %copy-start.2 = (bf16[512,224]{0,1:T(8,128)(2,1)S(1)}, bf16[512,224]{0,1:T(8,128)(2,1)}, u32[]{:S(2)}) copy-start(bf16[512,224]{0,1:T(8,128)(2,1)} %param.6) | copy-start | bytes 688132
  12.5 16.2 %copy-start.1 = (bf16[512,224]{0,1:T(8,128)(2,1)S(1)}, bf16[512,224]{0,1:T(8,128)(2,1)}, u32[]{:S(2)}) copy-start(bf16[512,224]{0,1:T(8,128)(2,1)} %param.7) | copy-start | bytes 688132
  13.4 16.2 %all-to-all-start = ((f32[8,32,112]{2,1,0:T(8,128)}), f32[8,32,112]{2,1,0:T(8,128)S(1)}, u32[]{:S(2)}, u32[]{:S(2)}) async-start(f32[8,32,112]{2,1,0:T(8,128)} %bitcast.6), calls=%async_computation | async-start | bytes 262144 | tf_op jit(solution)/shard_map/all_to_all | solution.py:19
  26.2 48.8 %all-gather.2.cloned.1.call-start = ((), (), s32[]{:S(2)}) async-start(), calls=%async_computation.5 | async-start | bytes 2580480 | tf_op jit(solution)/shard_map/all_gather | solution.py:63
  27.1 42.6 %copy-start.6 = (pred[512,512]{0,1:T(8,128)(4,1)}, pred[512,512]{0,1:T(8,128)(4,1)S(1)}, u32[]{:S(2)}) copy-start(pred[512,512]{0,1:T(8,128)(4,1)S(1)} %fusion.14) | copy-start | bytes 786436
  29.6 36.7 %copy-start.3 = (bf16[512,224]{0,1:T(8,128)(2,1)S(1)}, bf16[512,224]{0,1:T(8,128)(2,1)}, u32[]{:S(2)}) copy-start(bf16[512,224]{0,1:T(8,128)(2,1)} %param.8) | copy-start | bytes 688132
  29.6 11.7 %collective-permute-start = (f32[32,112]{1,0:T(8,128)S(1)}, f32[32,112]{1,0:T(8,128)S(1)}, u32[]{:S(2)}, u32[]{:S(2)}) collective-permute-start(f32[32,112]{1,0:T(8,128)S(1)} %get-tuple-element.11), channel_id=1, source_target_pairs={{0,64},{64,128},{128,192},{192,256},{256,320},{320,384},{384,448},... | collective-permute-start | bytes 43016 | tf_op jit(solution)/shard_map/ppermute | solution.py:15
  31.1 10.2 %collective-permute-start.1 = (f32[32,112]{1,0:T(8,128)S(1)}, f32[32,112]{1,0:T(8,128)S(1)}, u32[]{:S(2)}, u32[]{:S(2)}) collective-permute-start(f32[32,112]{1,0:T(8,128)S(1)} %get-tuple-element.11), channel_id=1, source_target_pairs={{0,128},{64,192},{128,256},{192,320},{256,384},{320,448},{384,512}... | collective-permute-start | bytes 43016 | tf_op jit(solution)/shard_map/ppermute | solution.py:15
  32.4 10.3 %collective-permute-start.2 = (f32[32,112]{1,0:T(8,128)S(1)}, f32[32,112]{1,0:T(8,128)S(1)}, u32[]{:S(2)}, u32[]{:S(2)}) collective-permute-start(f32[32,112]{1,0:T(8,128)S(1)} %get-tuple-element.11), channel_id=1, source_target_pairs={{0,192},{64,256},{128,320},{192,384},{256,448},{320,512},{384,576}... | collective-permute-start | bytes 43016 | tf_op jit(solution)/shard_map/ppermute | solution.py:15
  42.7 11.6 %collective-permute-start.3 = (f32[32,112]{1,0:T(8,128)S(1)}, f32[32,112]{1,0:T(8,128)S(1)}, u32[]{:S(2)}, u32[]{:S(2)}) collective-permute-start(f32[32,112]{1,0:T(8,128)S(1)} %fusion.49), channel_id=1, source_target_pairs={{0,256},{64,320},{128,384},{192,448},{256,512},{320,576},{384,640}... | collective-permute-start | bytes 43016 | tf_op jit(solution)/shard_map/ppermute | solution.py:15
  51.4 4.2 %collective-permute-start.4 = (f32[32,112]{1,0:T(8,128)S(1)}, f32[32,112]{1,0:T(8,128)S(1)}, u32[]{:S(2)}, u32[]{:S(2)}) collective-permute-start(f32[32,112]{1,0:T(8,128)S(1)} %fusion.49), channel_id=1, source_target_pairs={{0,512},{64,576},{128,640},{192,704},{1,513},{65,577},{129,641},{1... | collective-permute-start | bytes 43016 | tf_op jit(solution)/shard_map/ppermute | solution.py:15
  56.4 9.3 %all-to-all-start.1 = ((f32[8,32,112]{2,1,0:T(8,128)}), f32[8,32,112]{2,1,0:T(8,128)S(1)}, u32[]{:S(2)}, u32[]{:S(2)}) async-start(f32[8,32,112]{2,1,0:T(8,128)} %broadcast_add_fusion.1), calls=%async_computation.1 | async-start | bytes 262144 | tf_op jit(solution)/shard_map/all_to_all | solution.py:29
  78.7 8.2 %all-to-all-start.2 = ((f32[8,32,112]{2,1,0:T(8,128)}), f32[8,32,112]{2,1,0:T(8,128)S(1)}, u32[]{:S(2)}, u32[]{:S(2)}) async-start(f32[8,32,112]{2,1,0:T(8,128)} %bitcast.24), calls=%async_computation.3 | async-start | bytes 262144 | tf_op jit(solution)/shard_map/all_to_all | solution.py:19
  83.5 51.4 %reduce-scatter.2.cloned.1.call-start = ((), (), s32[]{:S(2)}) async-start(), calls=%async_computation.6 | async-start | bytes 2580480 | tf_op jit(solution)/shard_map/reduce_scatter | solution.py:90
  86.9 5.6 %collective-permute-start.5 = (f32[32,112]{1,0:T(8,128)S(1)}, f32[32,112]{1,0:T(8,128)S(1)}, u32[]{:S(2)}, u32[]{:S(2)}) collective-permute-start(f32[32,112]{1,0:T(8,128)S(1)} %get-tuple-element.8), channel_id=1, source_target_pairs={{64,0},{128,64},{192,128},{256,192},{320,256},{384,320},{448,384},... | collective-permute-start | bytes 43016 | tf_op jit(solution)/shard_map/ppermute | solution.py:15
  88.2 7.5 %collective-permute-start.6 = (f32[32,112]{1,0:T(8,128)S(1)}, f32[32,112]{1,0:T(8,128)S(1)}, u32[]{:S(2)}, u32[]{:S(2)}) collective-permute-start(f32[32,112]{1,0:T(8,128)S(1)} %get-tuple-element.8), channel_id=1, source_target_pairs={{128,0},{192,64},{256,128},{320,192},{384,256},{448,320},{512,384}... | collective-permute-start | bytes 43016 | tf_op jit(solution)/shard_map/ppermute | solution.py:15
  89.5 9.2 %collective-permute-start.7 = (f32[32,112]{1,0:T(8,128)S(1)}, f32[32,112]{1,0:T(8,128)S(1)}, u32[]{:S(2)}, u32[]{:S(2)}) collective-permute-start(f32[32,112]{1,0:T(8,128)S(1)} %get-tuple-element.8), channel_id=1, source_target_pairs={{192,0},{256,64},{320,128},{384,192},{448,256},{512,320},{576,384}... | collective-permute-start | bytes 43016 | tf_op jit(solution)/shard_map/ppermute | solution.py:15
  98.7 9.9 %collective-permute-start.8 = (f32[32,112]{1,0:T(8,128)S(1)}, f32[32,112]{1,0:T(8,128)S(1)}, u32[]{:S(2)}, u32[]{:S(2)}) collective-permute-start(f32[32,112]{1,0:T(8,128)S(1)} %fusion.50), channel_id=1, source_target_pairs={{256,0},{320,64},{384,128},{448,192},{512,256},{576,320},{640,384}... | collective-permute-start | bytes 43016 | tf_op jit(solution)/shard_map/ppermute | solution.py:15
  100.0 12.7 %collective-permute-start.9 = (f32[32,112]{1,0:T(8,128)S(1)}, f32[32,112]{1,0:T(8,128)S(1)}, u32[]{:S(2)}, u32[]{:S(2)}) collective-permute-start(f32[32,112]{1,0:T(8,128)S(1)} %fusion.50), channel_id=1, source_target_pairs={{512,0},{576,64},{640,128},{704,192},{513,1},{577,65},{641,129},{7... | collective-permute-start | bytes 43016 | tf_op jit(solution)/shard_map/ppermute | solution.py:15
  113.4 9.4 %all-to-all-start.3 = ((f32[8,32,112]{2,1,0:T(8,128)}), f32[8,32,112]{2,1,0:T(8,128)S(1)}, u32[]{:S(2)}, u32[]{:S(2)}) async-start(f32[8,32,112]{2,1,0:T(8,128)} %broadcast_add_fusion), calls=%async_computation.4 | async-start | bytes 262144 | tf_op jit(solution)/shard_map/all_to_all | solution.py:29
  121.3 3.3 %copy-start.4 = (bf16[512,224]{0,1:T(8,128)(2,1)S(1)}, bf16[512,224]{0,1:T(8,128)(2,1)}, u32[]{:S(2)}) copy-start(bf16[512,224]{0,1:T(8,128)(2,1)} %param.8) | copy-start | bytes 688132
  122.8 1.9 %copy-start.5 = (pred[512,224]{0,1:T(8,128)(4,1)S(1)}, pred[512,224]{0,1:T(8,128)(4,1)}, u32[]{:S(2)}) copy-start(pred[512,224]{0,1:T(8,128)(4,1)} %broadcast_compare_fusion) | copy-start | bytes 344068
  124.3 1.7 %copy-start.7 = (pred[512,512]{0,1:T(8,128)(4,1)S(1)}, pred[512,512]{0,1:T(8,128)(4,1)}, u32[]{:S(2)}) copy-start(pred[512,512]{0,1:T(8,128)(4,1)} %copy-done.6) | copy-start | bytes 786436
  (2 other events, 2.9 us)
Sparse Core Ops, SparseCore 0:
  29.4 45.5 all-gather.1
  88.0 46.8 reduce-scatter.1

commit v2 on v1

v2 whole, which is shorter than its diff:
```python
import jax
import jax.numpy as jnp
from jax import lax
from jax.experimental import pallas as pl
from jax.experimental.pallas import tpu as pltpu
from jax.sharding import Mesh
from jax.sharding import PartitionSpec as P

HD = 112
PAD = 128
PLANE = ("x", "c")
BF, F32 = jnp.bfloat16, jnp.float32
VMEM = pl.BlockSpec(memory_space=pltpu.VMEM)
SMEM = pl.BlockSpec(memory_space=pltpu.SMEM)
ANY = pl.BlockSpec(memory_space=pltpu.HBM)


def shape(dims, dtype):
    return jax.ShapeDtypeStruct(dims, dtype)


def call(body, outs, specs, name, cost=1000000):
    return pl.pallas_call(
        body,
        out_shape=outs,
        in_specs=specs,
        out_specs=jax.tree.map(lambda _: VMEM, outs),
        compiler_params=pltpu.CompilerParams(vmem_limit_bytes=40 * 1024 * 1024),
        cost_estimate=pl.CostEstimate(flops=cost, bytes_accessed=cost, transcendentals=0),
        name=name,
    )


def nn(a, b):
    return lax.dot_general(a, b, (((1,), (0,)), ((), ())), preferred_element_type=F32)


def nt(a, b):
    return lax.dot_general(a, b, (((1,), (1,)), ((), ())), preferred_element_type=F32)


def halves(x):
    top = x.astype(BF)
    return top, (x - top.astype(F32)).astype(BF)


def relu(x):
    return jnp.maximum(x, jnp.zeros_like(x))


def with_ones(v):
    row = lax.broadcasted_iota(jnp.int32, (PAD - HD, v.shape[1]), 0)
    return jnp.concatenate([v, (row < 2).astype(F32).astype(BF)], axis=0)


def taller(x):
    return jnp.concatenate([x, jnp.zeros((PAD - HD, x.shape[1]), x.dtype)], axis=0)


def live_row(live, n):
    return lax.broadcasted_iota(jnp.int32, (1, n), 1) < live


def causal(rows, cols, row0):
    t = lax.broadcasted_iota(jnp.int32, (rows, cols), 0) + row0
    return t >= lax.broadcasted_iota(jnp.int32, (rows, cols), 1)


def rows_of(h):
    return slice(h * HD, (h + 1) * HD)


def state_kernel(live_ref, k_ref, v_ref, out_ref):
    n = k_ref.shape[1]
    ok = live_row(live_ref[0], n)
    for h in range(k_ref.shape[0] // HD):
        fk = jnp.where(ok, relu(k_ref[rows_of(h)]).astype(F32), 0.0).astype(BF)
        out_ref[h * PAD : (h + 1) * PAD] = nt(with_ones(v_ref[rows_of(h)]), taller(fk))


def total_kernel(mine_ref, out_ref):
    total = jnp.sum(mine_ref[...], axis=0).astype(BF)
    for i in range(out_ref.shape[0]):
        out_ref[i] = total


def spread_kernel(sign, z_ref, mine_ref, all_ref, out_ref):
    z = z_ref[0]
    base = jnp.zeros(mine_ref.shape[1:], F32)
    for i in range(all_ref.shape[0]):
        keep = (i < z) if sign > 0 else (i > z)
        base = base + jnp.where(keep, all_ref[i].astype(F32), 0.0)
    steps = range(mine_ref.shape[0])
    for i in steps if sign > 0 else reversed(steps):
        out_ref[i] = base
        base = base + mine_ref[i]


def sums_beyond(packed, z, sign):
    count = lax.axis_size("z")
    rows = packed.shape[0] // 8
    mine = lax.all_to_all(packed.reshape(8, rows, PAD), PLANE, 0, 0)
    totals = call(total_kernel, shape((count, rows, PAD), BF), [VMEM], "plane_total")(mine)
    everyone = lax.all_to_all(totals, "z", 0, 0)
    back = call(
        lambda *refs: spread_kernel(sign, *refs), shape((8, rows, PAD), F32), [SMEM, VMEM, VMEM], "spread"
    )(z, mine, everyone)
    return lax.all_to_all(back, PLANE, 0, 0).reshape(8 * rows, PAD)


def weights_kernel(q_ref, k_ref, v_ref, w_ref, num_ref):
    n = q_ref.shape[1]
    half = n // 2
    for h in range(q_ref.shape[0] // HD):
        fq = relu(q_ref[rows_of(h)])
        fk = relu(k_ref[rows_of(h)])
        va = with_ones(v_ref[rows_of(h)])
        fqt = taller(fq).astype(F32).T.astype(BF)
        fk = taller(fk)
        for i in range(2):
            cols = half * (i + 1)
            s = nn(fqt[i * half : (i + 1) * half], fk[:, :cols])
            w = jnp.where(causal(half, cols, i * half), s, 0.0).astype(BF)
            w_ref[h, i * half : (i + 1) * half, :cols] = w
            if i == 0:
                w_ref[h, :half, half:] = jnp.zeros((half, half), BF)
            num_ref[h * PAD : (h + 1) * PAD, i * half : (i + 1) * half] = nt(va[:, :cols], w)


def attend_kernel(live_ref, q_ref, num_ref, st_ref, attn_ref, numer_ref):
    n = q_ref.shape[1]
    ok = live_row(live_ref[0], n)
    for h in range(q_ref.shape[0] // HD):
        at = slice(h * PAD, (h + 1) * PAD)
        fq = taller(relu(q_ref[rows_of(h)]))
        top, low = halves(st_ref[at])
        numer = num_ref[at] + (nn(top, fq) + nn(low, fq))
        numer_ref[at] = numer
        inv = 1.0 / (numer[HD : HD + 1] + 1.0)
        attn_ref[rows_of(h)] = jnp.where(ok, numer[:HD] * inv, 0.0).astype(BF)


def adjoint_kernel(live_ref, cot_ref, proj_ref, q_ref, numer_ref, after_ref, dn_ref, adj_ref):
    n = q_ref.shape[1]
    ok = live_row(live_ref[0], n)
    grad = nn(proj_ref[...], cot_ref[...]).astype(BF).astype(F32)
    row = lax.broadcasted_iota(jnp.int32, (PAD - HD, n), 0)
    for h in range(q_ref.shape[0] // HD):
        at = slice(h * PAD, (h + 1) * PAD)
        numer = numer_ref[at]
        inv = 1.0 / (numer[HD : HD + 1] + 1.0)
        g = grad[rows_of(h)]
        dn = jnp.where(ok, g * inv, 0.0).astype(BF)
        dd = jnp.where(ok, -jnp.sum(g * numer[:HD], axis=0, keepdims=True) * inv * inv, 0.0)
        top = dd.astype(BF).astype(F32)
        tail = jnp.where(row == 0, top, jnp.where(row == 1, dd - top, 0.0)).astype(BF)
        dna = jnp.concatenate([dn, tail], axis=0)
        dn_ref[at] = dna
        adj_ref[at] = nt(taller(relu(q_ref[rows_of(h)])), dna)


def local_grad_kernel(live_ref, q_ref, k_ref, v_ref, w_ref, dn_ref, st_ref, gq_ref, gk_ref, gv_ref):
    n = q_ref.shape[1]
    half = n // 2
    ok = live_row(live_ref[0], n)
    for h in range(q_ref.shape[0] // HD):
        at = slice(h * PAD, (h + 1) * PAD)
        q = q_ref[rows_of(h)]
        fq = relu(q)
        fk = relu(k_ref[rows_of(h)])
        va = with_ones(v_ref[rows_of(h)])
        dna = dn_ref[at]
        dnt = dna.astype(F32).T.astype(BF)
        d0 = jnp.where(causal(half, half, 0), nn(dnt[:half], va[:, :half]), 0.0).astype(BF)
        d1 = jnp.where(causal(half, n, half), nn(dnt[half:], va), 0.0).astype(BF)
        st = st_ref[at].T
        top, low = halves(st)
        dd = dna[HD : HD + 1].astype(F32) + dna[HD + 1 : HD + 2].astype(F32)
        bare = jnp.concatenate([dna[:HD], jnp.zeros((PAD - HD, n), BF)], axis=0)
        gq = jnp.concatenate([nt(fk[:, :half], d0), nt(fk, d1)], axis=1)
        gq = gq + (nn(top, bare) + nn(low, bare))[:HD] + st[:HD, HD : HD + 1] * dd
        gq_ref[rows_of(h)] = jnp.where(ok & (q.astype(F32) > 0), gq, 0.0).astype(BF)
        gk = nn(fq[:, half:], d1)
        gk_ref[rows_of(h), half:] = gk[:, half:]
        gk_ref[rows_of(h), :half] = gk[:, :half] + nn(fq[:, :half], d0)
        gv_ref[rows_of(h)] = nn(dna[:HD], w_ref[h])


def far_grad_kernel(live_ref, k_ref, v_ref, gk_ref, gv_ref, adj_ref, outk_ref, outv_ref):
    n = k_ref.shape[1]
    ok = live_row(live_ref[0], n)
    for h in range(k_ref.shape[0] // HD):
        adj = adj_ref[h * PAD : (h + 1) * PAD]
        k = k_ref[rows_of(h)]
        fk = taller(relu(k))
        va = with_ones(v_ref[rows_of(h)])
        top, low = halves(adj)
        gk = gk_ref[rows_of(h)] + (nn(top, va) + nn(low, va))[:HD]
        outk_ref[rows_of(h)] = jnp.where(ok & (k.astype(F32) > 0), gk, 0.0).astype(BF)
        top, low = halves(adj.T)
        gv = gv_ref[rows_of(h)] + (nn(top, fk) + nn(low, fk))[:HD]
        outv_ref[rows_of(h)] = jnp.where(ok, gv, 0.0).astype(BF)


def per_device(query, key_in, value, proj, cot, lengths):
    q, k, v = query.T, key_in.T, value.T
    width, n = q.shape
    heads = width // HD
    live = lax.dynamic_slice(lengths, (lax.axis_index(("z", "x", "c")),), (1,))
    z = lax.axis_index("z").astype(jnp.int32).reshape(1)
    cot_all = lax.all_gather(cot, "y", axis=0, tiled=True)
    packed = call(state_kernel, shape((heads * PAD, PAD), F32), [SMEM, VMEM, VMEM], "own_state")(live, k, v)
    state = sums_beyond(packed, z, 1)
    w, num = call(
        weights_kernel,
        (shape((heads, n, n), BF), shape((heads * PAD, n), F32)),
        [VMEM] * 3,
        "own_weights",
    )(q, k, v)
    attn, numer = call(
        attend_kernel,
        (shape((width, n), BF), shape((heads * PAD, n), F32)),
        [SMEM] + [VMEM] * 3,
        "attend",
    )(live, q, num, state)
    terms = lax.dot_general(proj, attn, (((0,), (0,)), ((), ())), preferred_element_type=F32).astype(BF)
    mixed = lax.psum_scatter(terms, "y", scatter_dimension=0, tiled=True)
    dn, adj = call(
        adjoint_kernel,
        (shape((heads * PAD, n), BF), shape((heads * PAD, PAD), F32)),
        [SMEM] + [VMEM] * 4 + [ANY],
        "own_adjoint",
    )(live, cot_all, proj, q, numer, terms)
    adj_next = sums_beyond(adj, z, -1)
    gq, gk, gv = call(
        local_grad_kernel,
        (shape((width, n), BF), shape((width, n), F32), shape((width, n), F32)),
        [SMEM] + [VMEM] * 6,
        "own_gradients",
    )(live, q, k, v, w, dn, state)
    gk, gv = call(
        far_grad_kernel,
        (shape((width, n), BF), shape((width, n), BF)),
        [SMEM] + [VMEM] * 5,
        "far_gradients",
    )(live, k, v, gk, gv, adj_next)
    return mixed, gq.T, gk.T, gv.T


def solution(mesh):
    group, head = mesh.devices.shape
    fine = Mesh(mesh.devices.reshape(group // 8, 4, 2, head), ("z", "x", "c", "y"))
    tokens = ("z", "x", "c")
    return jax.shard_map(
        per_device,
        mesh=fine,
        in_specs=(P(tokens, "y"), P(tokens, "y"), P(tokens, "y"), P("y", None), P("y", tokens), P()),
        out_specs=(P("y", tokens), P(tokens, "y"), P(tokens, "y"), P(tokens, "y")),
        check_vma=False,
    )
```

time: 143 us -> 123 us (0.86)
  blocking collectives: 0 us -> 65.1 us
  starting transfers between devices: 59.1 us -> 11.6 us
  waiting for transfers between devices: 41.5 us -> 3.77 us
  matrix products: 16.5 us -> 2.27 us
  local copies, waits for them, and re-layouts: 2.49 us -> 14.5 us
  Pallas kernels: 0 us -> 9.87 us
  other arithmetic: 7.63 us -> 0 us
    all_to_all x0 -> x4, blocking collectives: none -> 65.1 us  [the longest x2 41.6 us: sums_beyond(): everyone = lax.all_to_all(totals, 'z', 0, 0)]
    ppermute x10 -> x0, starting transfers between devices: 29.6 us -> none  [shifted(): return lax.ppermute(block, 'z', route)]
    ppermute x10 -> x0, waiting for transfers between devices: 22 us -> none  [shifted(): return lax.ppermute(block, 'z', route)]
    all_to_all x4 -> x2, starting transfers between devices: 29.5 us -> 11.6 us  [sums_beyond(): return lax.all_to_all(back, PLANE, 0, 0).reshape(8 * rows, PAD)]
    dot_general x18 -> x1, matrix products: 16.5 us -> 2.27 us  [per_device(): lax.dot_general(proj, attn, (((0,), (0,)), ((), ())), preferred_element_t...]
    unnamed x27 -> x40, local copies, waits for them, and re-layouts: 0.73 us -> 13.2 us
    pallas_call x0 -> x10, Pallas kernels: none -> 9.87 us  [the longest x1 2.37 us: per_device(): call(local_grad_kernel, (shape((width, n), BF), shape((width, n), F32), s...]
    reduce_scatter x1, waiting for transfers between devices: 7.74 us -> 0.41 us  [per_device(): mixed = lax.psum_scatter(terms, 'y', scatter_dimension=0, tiled=True)]
  transfers between devices with their start and end apart: 16 -> 4, of which waited for: 13 -> 2; matrix products, arithmetic and copies ran while one was open for 11% -> 3% of each run, Pallas kernels for 0% -> 8%
where the time goes in v2:
time: 123 us; the launch traced here: 121 us
  blocking collectives  65.1 us (53%)
  local copies, waits for them, and re-layouts  14.5 us (12%)
  between operations  14.2 us (12%)
  starting transfers between devices  11.6 us (9%)
  Pallas kernels  9.87 us (8%)
  waiting for transfers between devices  3.77 us (3%)
  matrix products  2.27 us (2%)
    all_to_all x2, blocking collectives, sums_beyond(): everyone = lax.all_to_all(totals, 'z', 0, 0)  41.6 us
    all_to_all x2, blocking collectives, sums_beyond(): mine = lax.all_to_all(packed.reshape(8, rows, PAD), PLANE, 0, 0)  23.5 us
    unnamed x40, local copies, waits for them, and re-layouts  13.2 us
    all_to_all x2, starting transfers between devices, sums_beyond(): return lax.all_to_all(back, PLANE, 0, 0).reshape(8 * rows, PAD)  11.6 us
    all_gather x1, waiting for transfers between devices, per_device(): cot_all = lax.all_gather(cot, 'y', axis=0, tiled=True)  2.65 us
  transfers between devices with their start and end apart: 4, of which 2 were waited for; matrix products, arithmetic and copies ran while one was open for 3% of the time, Pallas kernels for 8%

profile of v2, /device:TPU:4, one launch (start us, length us, event | category | flops | bytes accessed | tf_op | source)
XLA Modules:
  0.0 121.3 jit_solution(2229391066996968669)
XLA Ops:
  7.9 1.3 %dynamic_slice.3.live_ref = s32[1]{0:T(128)} dynamic-slice(s32[96]{0:T(128)} %param.11, s32[]{:T(128)S(6)} %select_n.3), dynamic_slice_sizes={1} | dynamic-slice | bytes 12 | tf_op jit(solution)/shard_map/dynamic_slice | solution.py:209
  9.2 0.9 copy-done.3
  10.1 0.9 copy-done.7
  11.9 15.3 %all_to_all.30.mine_ref.refs_1_ = f32[8,32,128]{2,1,0:T(8,128)S(1)} all-to-all(f32[8,32,128]{2,1,0:T(8,128)S(1)} %bitcast.29), channel_id=1, replica_groups=mesh['z'=12,'x'=4,'c'=2,'y'=8] {'x','c'}, dimensions={0} | all-to-all | bytes 262144 | tf_op jit(solution)/shard_map/all_to_all | solution.py:102
  27.3 19.7 %all_to_all.31.refs_2_ = bf16[12,32,128]{2,1,0:T(8,128)(2,1)S(1)} all-to-all(bf16[12,32,128]{2,1,0:T(8,128)(2,1)S(1)} %plane_total.2), channel_id=1, replica_groups=mesh['z'=12,'x'=4,'c'=2,'y'=8] {'z'}, dimensions={0} | all-to-all | bytes 196608 | tf_op jit(solution)/shard_map/all_to_all | solution.py:104
  47.6 5.8 %all-to-all-start.2 = ((f32[8,32,128]{2,1,0:T(8,128)}), f32[8,32,128]{2,1,0:T(8,128)S(1)}, u32[]{:S(2)}, u32[]{:S(2)}) async-start(f32[8,32,128]{2,1,0:T(8,128)} %spread.2), calls=%async_computation.2 | async-start | bytes 262144 | tf_op jit(solution)/shard_map/all_to_all | solution.py:108
  53.4 0.9 copy-done.4
  54.4 0.9 copy-done.8
  56.2 1.0 copy-done.14
  57.2 0.9 attend.1
  59.0 2.3 %fusion.after_ref = bf16[2240,512]{1,0:T(8,128)(2,1)} fusion(bf16[224,512]{1,0:T(8,128)(2,1)S(1)} %get-tuple-element.16, bf16[224,2240]{1,0:T(8,128)(2,1)S(1)} %copy-done.1), kind=kOutput, calls=%fused_computation.1 | convolution fusion | flops 514949120 | bytes 3526656 | tf_op jit(solution)/shard_map/dot_general | solution.py:226
  61.3 2.7 %all-gather.2.cloned.1.call-done.cot_ref = bf16[2240,512]{1,0:T(8,128)(2,1)} async-done(((bf16[280,512]{1,0:T(8,128)(2,1)}), bf16[2240,512]{1,0:T(8,128)(2,1)}) %all-gather.2.cloned.1.call-update) | async-done | bytes 2293776 | tf_op jit(solution)/shard_map/all_gather | solution.py:211
  64.0 1.6 %copy-done.11 = bf16[2240,512]{1,0:T(8,128)(2,1)S(1)} copy-done((bf16[2240,512]{1,0:T(8,128)(2,1)S(1)}, bf16[2240,512]{1,0:T(8,128)(2,1)}, u32[]{:S(2)}) %copy-start.11) | copy-done | bytes 2293784
  65.6 1.0 copy-done.17
  66.6 1.6 %own_adjoint.1 = (bf16[256,512]{1,0:T(8,128)(2,1)S(1)}, f32[256,128]{1,0:T(8,128)S(1)}) custom-call(s32[1]{0:T(128)} %dynamic_slice.3.live_ref, bf16[2240,512]{1,0:T(8,128)(2,1)S(1)} %copy-done.11, bf16[224,2240]{1,0:T(8,128)(2,1)S(1)} %copy-done.1, bf16[224,512]{1,0:T(8,128)(2,1)S(1)} %bitcast.17, f32[256,512]{1,0:T(8,128)S(1)} %copy-done.17, ...), custom_call_target="tpu_custom_call" | custom-call | flops 1000000 | bytes 1000000 | tf_op jit(solution)/shard_map/own_adjoint/pallas_call | solution.py:228
  68.3 8.2 %all_to_all.32.mine_ref.refs_1_ = f32[8,32,128]{2,1,0:T(8,128)S(1)} all-to-all(f32[8,32,128]{2,1,0:T(8,128)S(1)} %bitcast.31), channel_id=1, replica_groups=mesh['z'=12,'x'=4,'c'=2,'y'=8] {'x','c'}, dimensions={0} | all-to-all | bytes 262144 | tf_op jit(solution)/shard_map/all_to_all | solution.py:102
  76.4 22.0 %all_to_all.33.refs_2_ = bf16[12,32,128]{2,1,0:T(8,128)(2,1)S(1)} all-to-all(bf16[12,32,128]{2,1,0:T(8,128)(2,1)S(1)} %plane_total.3), channel_id=1, replica_groups=mesh['z'=12,'x'=4,'c'=2,'y'=8] {'z'}, dimensions={0} | all-to-all | bytes 196608 | tf_op jit(solution)/shard_map/all_to_all | solution.py:104
  99.1 5.8 %all-to-all-start.5 = ((f32[8,32,128]{2,1,0:T(8,128)}), f32[8,32,128]{2,1,0:T(8,128)S(1)}, u32[]{:S(2)}, u32[]{:S(2)}) async-start(f32[8,32,128]{2,1,0:T(8,128)} %spread.3), calls=%async_computation.6 | async-start | bytes 262144 | tf_op jit(solution)/shard_map/all_to_all | solution.py:108
  104.9 0.9 copy-done.5
  105.8 0.9 copy-done.9
  107.7 1.2 %copy-done.15 = bf16[2,512,512]{2,1,0:T(8,128)(2,1)S(1)} copy-done((bf16[2,512,512]{2,1,0:T(8,128)(2,1)S(1)}, bf16[2,512,512]{2,1,0:T(8,128)(2,1)}, u32[]{:S(2)}) %copy-start.15) | copy-done | bytes 1048600
  108.9 1.0 copy-done.19
  109.9 2.4 %own_gradients.1 = (bf16[224,512]{1,0:T(8,128)(2,1)}, f32[224,512]{1,0:T(8,128)S(1)}, f32[224,512]{1,0:T(8,128)S(1)}) custom-call(s32[1]{0:T(128)} %dynamic_slice.3.live_ref, bf16[224,512]{1,0:T(8,128)(2,1)S(1)} %bitcast.18, bf16[224,512]{1,0:T(8,128)(2,1)S(1)} %bitcast.21, bf16[224,512]{1,0:T(8,128)(2,1)S(1)} %bitcast.25, ...), custom_call_target="tpu_custom_call" | custom-call | flops 1000000 | bytes 1000000 | tf_op jit(solution)/shard_map/own_gradients/pallas_call | solution.py:235
  112.2 1.8 %far_gradients.1 = (bf16[224,512]{1,0:T(8,128)(2,1)}, bf16[224,512]{1,0:T(8,128)(2,1)}) custom-call(s32[1]{0:T(128)} %dynamic_slice.3.live_ref, bf16[224,512]{1,0:T(8,128)(2,1)S(1)} %bitcast.22, bf16[224,512]{1,0:T(8,128)(2,1)S(1)} %bitcast.26, f32[224,512]{1,0:T(8,128)S(1)} %get-tuple-element.21.gk_ref, f32[224,512]{1,0:T(8,128)S(1)} %get-tuple-element.22.gv_ref, ...), custom_call_target="tpu_custom_call" | custom-call | flops 1000000 | bytes 1000000 | tf_op jit(solution)/shard_map/far_gradients/pallas_call | solution.py:241
  (42 shorter events, 6.1 us)
Async XLA Ops:
  7.2 46.2 %copy-start.2 = (bf16[512,224]{0,1:T(8,128)(2,1)S(1)}, bf16[512,224]{0,1:T(8,128)(2,1)}, u32[]{:S(2)}) copy-start(bf16[512,224]{0,1:T(8,128)(2,1)} %param.6) | copy-start | bytes 688132
  7.2 51.8 %copy-start.1 = (bf16[224,2240]{1,0:T(8,128)(2,1)S(1)}, bf16[224,2240]{1,0:T(8,128)(2,1)}, u32[]{:S(2)}) copy-start(bf16[224,2240]{1,0:T(8,128)(2,1)} %proj_ref.1) | copy-start | bytes 3010564
  7.2 56.8 %all-gather.2.cloned.1.call-start = ((), (), s32[]{:S(2)}) async-start(), calls=%async_computation.8 | async-start | bytes 2580480 | tf_op jit(solution)/shard_map/all_gather | solution.py:211
  9.2 0.9 copy-start.3
  10.1 0.9 copy-start.7
  47.6 9.6 %all-to-all-start.2 = ((f32[8,32,128]{2,1,0:T(8,128)}), f32[8,32,128]{2,1,0:T(8,128)S(1)}, u32[]{:S(2)}, u32[]{:S(2)}) async-start(f32[8,32,128]{2,1,0:T(8,128)} %spread.2), calls=%async_computation.2 | async-start | bytes 262144 | tf_op jit(solution)/shard_map/all_to_all | solution.py:108
  53.4 61.1 %reduce-scatter.2.cloned.1.call-start = ((), (), s32[]{:S(2)}) async-start(), calls=%async_computation.7 | async-start | bytes 2580480 | tf_op jit(solution)/shard_map/reduce_scatter | solution.py:227
  53.4 0.9 copy-start.4
  54.4 0.9 copy-start.8
  56.2 1.0 copy-start.14
  57.2 1.8 %copy-start.12 = (f32[8,32,128]{2,1,0:T(8,128)}, f32[8,32,128]{2,1,0:T(8,128)S(1)}, u32[]{:S(2)}) copy-start(f32[8,32,128]{2,1,0:T(8,128)S(1)} %all-to-all-done.2) | copy-start | bytes 393220
  58.2 0.8 copy-start.16
  61.3 2.7 %copy-start = (bf16[2240,512]{1,0:T(8,128)(2,1)S(1)}, bf16[2240,512]{1,0:T(8,128)(2,1)}, u32[]{:S(2)}) copy-start(bf16[2240,512]{1,0:T(8,128)(2,1)} %fusion.after_ref) | copy-start | bytes 6881284
  63.9 1.6 %copy-start.11 = (bf16[2240,512]{1,0:T(8,128)(2,1)S(1)}, bf16[2240,512]{1,0:T(8,128)(2,1)}, u32[]{:S(2)}) copy-start(bf16[2240,512]{1,0:T(8,128)(2,1)} %all-gather.2.cloned.1.call-done.cot_ref) | copy-start | bytes 6881284
  65.6 1.0 copy-start.17
  68.2 30.2 %copy-start.18 = (bf16[256,512]{1,0:T(8,128)(2,1)}, bf16[256,512]{1,0:T(8,128)(2,1)S(1)}, u32[]{:S(2)}) copy-start(bf16[256,512]{1,0:T(8,128)(2,1)S(1)} %get-tuple-element.19.dn_ref) | copy-start | bytes 786436
  68.2 44.0 %copy-start.6 = (bf16[512,224]{0,1:T(8,128)(2,1)S(1)}, bf16[512,224]{0,1:T(8,128)(2,1)}, u32[]{:S(2)}) copy-start(bf16[512,224]{0,1:T(8,128)(2,1)} %param.7) | copy-start | bytes 688132
  68.2 44.0 %copy-start.10 = (bf16[512,224]{0,1:T(8,128)(2,1)S(1)}, bf16[512,224]{0,1:T(8,128)(2,1)}, u32[]{:S(2)}) copy-start(bf16[512,224]{0,1:T(8,128)(2,1)} %param.8) | copy-start | bytes 688132
  99.1 13.1 %all-to-all-start.5 = ((f32[8,32,128]{2,1,0:T(8,128)}), f32[8,32,128]{2,1,0:T(8,128)S(1)}, u32[]{:S(2)}, u32[]{:S(2)}) async-start(f32[8,32,128]{2,1,0:T(8,128)} %spread.3), calls=%async_computation.6 | async-start | bytes 262144 | tf_op jit(solution)/shard_map/all_to_all | solution.py:108
  104.9 0.9 copy-start.5
  105.8 0.9 copy-start.9
  106.8 0.9 copy-start.13
  107.7 1.2 %copy-start.15 = (bf16[2,512,512]{2,1,0:T(8,128)(2,1)S(1)}, bf16[2,512,512]{2,1,0:T(8,128)(2,1)}, u32[]{:S(2)}) copy-start(bf16[2,512,512]{2,1,0:T(8,128)(2,1)} %copy-done.14) | copy-start | bytes 3145732
  108.9 1.0 copy-start.19
Sparse Core Ops, SparseCore 0:
  10.4 53.5 all-gather.1
  67.7 46.7 reduce-scatter.1

commit v3 on v2

--- a/solution.py
+++ b/solution.py
@@ -12,7 +12,8 @@
 BF, F32 = jnp.bfloat16, jnp.float32
 VMEM = pl.BlockSpec(memory_space=pltpu.VMEM)
 SMEM = pl.BlockSpec(memory_space=pltpu.SMEM)
-ANY = pl.BlockSpec(memory_space=pltpu.HBM)
+STEP = 640
+LIMIT = 16 * 1024 * 1024
 
 
 def shape(dims, dtype):
@@ -25,7 +26,7 @@
         out_shape=outs,
         in_specs=specs,
         out_specs=jax.tree.map(lambda _: VMEM, outs),
-        compiler_params=pltpu.CompilerParams(vmem_limit_bytes=40 * 1024 * 1024),
+        compiler_params=pltpu.CompilerParams(vmem_limit_bytes=LIMIT),
         cost_estimate=pl.CostEstimate(flops=cost, bytes_accessed=cost, transcendentals=0),
         name=name,
     )
@@ -57,8 +58,8 @@
     return jnp.concatenate([x, jnp.zeros((PAD - HD, x.shape[1]), x.dtype)], axis=0)
 
 
-def live_row(live, n):
-    return lax.broadcasted_iota(jnp.int32, (1, n), 1) < live
+def live_row(place_ref, lengths_ref, n):
+    return lax.broadcasted_iota(jnp.int32, (1, n), 1) < lengths_ref[place_ref[0]]
 
 
 def causal(rows, cols, row0):
@@ -70,15 +71,15 @@
     return slice(h * HD, (h + 1) * HD)
 
 
-def state_kernel(live_ref, k_ref, v_ref, out_ref):
+def state_kernel(place_ref, lengths_ref, k_ref, v_ref, out_ref):
     n = k_ref.shape[1]
-    ok = live_row(live_ref[0], n)
+    ok = live_row(place_ref, lengths_ref, n)
     for h in range(k_ref.shape[0] // HD):
         fk = jnp.where(ok, relu(k_ref[rows_of(h)]).astype(F32), 0.0).astype(BF)
         out_ref[h * PAD : (h + 1) * PAD] = nt(with_ones(v_ref[rows_of(h)]), taller(fk))
 
 
-def total_kernel(mine_ref, out_ref):
+def total_kernel(mine_ref, after_ref, out_ref):
     total = jnp.sum(mine_ref[...], axis=0).astype(BF)
     for i in range(out_ref.shape[0]):
         out_ref[i] = total
@@ -96,11 +97,11 @@
         base = base + mine_ref[i]
 
 
-def sums_beyond(packed, z, sign):
+def sums_beyond(packed, z, sign, after):
     count = lax.axis_size("z")
     rows = packed.shape[0] // 8
     mine = lax.all_to_all(packed.reshape(8, rows, PAD), PLANE, 0, 0)
-    totals = call(total_kernel, shape((count, rows, PAD), BF), [VMEM], "plane_total")(mine)
+    totals = call(total_kernel, shape((count, rows, PAD), BF), [VMEM] * 2, "plane_total")(mine, after)
     everyone = lax.all_to_all(totals, "z", 0, 0)
     back = call(
         lambda *refs: spread_kernel(sign, *refs), shape((8, rows, PAD), F32), [SMEM, VMEM, VMEM], "spread"
@@ -108,28 +109,32 @@
     return lax.all_to_all(back, PLANE, 0, 0).reshape(8 * rows, PAD)
 
 
-def weights_kernel(q_ref, k_ref, v_ref, w_ref, num_ref):
+def weights_of(fq, fk, half, i):
+    cols = half * (i + 1)
+    fqt = taller(fq[:, i * half : (i + 1) * half]).astype(F32).T.astype(BF)
+    s = nn(fqt, taller(fk)[:, :cols])
+    return jnp.where(causal(half, cols, i * half), s, 0.0).astype(BF)
+
+
+def weights_kernel(q_ref, k_ref, v_ref, num_ref, token_ref):
+    token_ref[...] = jnp.zeros(token_ref.shape, F32)
     n = q_ref.shape[1]
     half = n // 2
     for h in range(q_ref.shape[0] // HD):
         fq = relu(q_ref[rows_of(h)])
         fk = relu(k_ref[rows_of(h)])
         va = with_ones(v_ref[rows_of(h)])
-        fqt = taller(fq).astype(F32).T.astype(BF)
-        fk = taller(fk)
         for i in range(2):
-            cols = half * (i + 1)
-            s = nn(fqt[i * half : (i + 1) * half], fk[:, :cols])
-            w = jnp.where(causal(half, cols, i * half), s, 0.0).astype(BF)
-            w_ref[h, i * half : (i + 1) * half, :cols] = w
-            if i == 0:
-                w_ref[h, :half, half:] = jnp.zeros((half, half), BF)
-            num_ref[h * PAD : (h + 1) * PAD, i * half : (i + 1) * half] = nt(va[:, :cols], w)
-
-
-def attend_kernel(live_ref, q_ref, num_ref, st_ref, attn_ref, numer_ref):
-    n = q_ref.shape[1]
-    ok = live_row(live_ref[0], n)
+            w = weights_of(fq, fk, half, i)
+            num_ref[h * PAD : (h + 1) * PAD, i * half : (i + 1) * half] = nt(va[:, : half * (i + 1)], w)
+
+
+def attend_kernel(
+    place_ref, lengths_ref, q_ref, num_ref, st_ref, proj_ref, terms_ref, numer_ref, token_ref
+):
+    n = q_ref.shape[1]
+    ok = live_row(place_ref, lengths_ref, n)
+    attn = []
     for h in range(q_ref.shape[0] // HD):
         at = slice(h * PAD, (h + 1) * PAD)
         fq = taller(relu(q_ref[rows_of(h)]))
@@ -137,12 +142,18 @@
         numer = num_ref[at] + (nn(top, fq) + nn(low, fq))
         numer_ref[at] = numer
         inv = 1.0 / (numer[HD : HD + 1] + 1.0)
-        attn_ref[rows_of(h)] = jnp.where(ok, numer[:HD] * inv, 0.0).astype(BF)
-
-
-def adjoint_kernel(live_ref, cot_ref, proj_ref, q_ref, numer_ref, after_ref, dn_ref, adj_ref):
-    n = q_ref.shape[1]
-    ok = live_row(live_ref[0], n)
+        attn.append(jnp.where(ok, numer[:HD] * inv, 0.0).astype(BF))
+    attn = jnp.concatenate(attn, axis=0)
+    features = proj_ref.shape[1]
+    for start in range(0, features, STEP):
+        part = slice(start, min(start + STEP, features))
+        terms_ref[part] = nn(proj_ref[:, part].astype(F32).T.astype(BF), attn).astype(BF)
+    token_ref[...] = jnp.zeros(token_ref.shape, F32)
+
+
+def adjoint_kernel(place_ref, lengths_ref, cot_ref, proj_ref, q_ref, numer_ref, after_ref, dn_ref, adj_ref):
+    n = q_ref.shape[1]
+    ok = live_row(place_ref, lengths_ref, n)
     grad = nn(proj_ref[...], cot_ref[...]).astype(BF).astype(F32)
     row = lax.broadcasted_iota(jnp.int32, (PAD - HD, n), 0)
     for h in range(q_ref.shape[0] // HD):
@@ -159,10 +170,11 @@
         adj_ref[at] = nt(taller(relu(q_ref[rows_of(h)])), dna)
 
 
-def local_grad_kernel(live_ref, q_ref, k_ref, v_ref, w_ref, dn_ref, st_ref, gq_ref, gk_ref, gv_ref):
+def local_grad_kernel(place_ref, lengths_ref, q_ref, k_ref, v_ref, dn_ref, st_ref, gq_ref, gk_ref, gv_ref, token_ref):
+    token_ref[...] = jnp.zeros(token_ref.shape, F32)
     n = q_ref.shape[1]
     half = n // 2
-    ok = live_row(live_ref[0], n)
+    ok = live_row(place_ref, lengths_ref, n)
     for h in range(q_ref.shape[0] // HD):
         at = slice(h * PAD, (h + 1) * PAD)
         q = q_ref[rows_of(h)]
@@ -183,12 +195,14 @@
         gk = nn(fq[:, half:], d1)
         gk_ref[rows_of(h), half:] = gk[:, half:]
         gk_ref[rows_of(h), :half] = gk[:, :half] + nn(fq[:, :half], d0)
-        gv_ref[rows_of(h)] = nn(dna[:HD], w_ref[h])
-
-
-def far_grad_kernel(live_ref, k_ref, v_ref, gk_ref, gv_ref, adj_ref, outk_ref, outv_ref):
+        gv = nn(dna[:HD, half:], weights_of(fq, fk, half, 1))
+        gv_ref[rows_of(h), half:] = gv[:, half:]
+        gv_ref[rows_of(h), :half] = gv[:, :half] + nn(dna[:HD, :half], weights_of(fq, fk, half, 0))
+
+
+def far_grad_kernel(place_ref, lengths_ref, k_ref, v_ref, gk_ref, gv_ref, adj_ref, outk_ref, outv_ref):
     n = k_ref.shape[1]
-    ok = live_row(live_ref[0], n)
+    ok = live_row(place_ref, lengths_ref, n)
     for h in range(k_ref.shape[0] // HD):
         adj = adj_ref[h * PAD : (h + 1) * PAD]
         k = k_ref[rows_of(h)]
@@ -206,44 +220,39 @@
     q, k, v = query.T, key_in.T, value.T
     width, n = q.shape
     heads = width // HD
-    live = lax.dynamic_slice(lengths, (lax.axis_index(("z", "x", "c")),), (1,))
+    place = lax.axis_index(("z", "x", "c")).astype(jnp.int32).reshape(1)
+    token = shape((8, 128), F32)
     z = lax.axis_index("z").astype(jnp.int32).reshape(1)
     cot_all = lax.all_gather(cot, "y", axis=0, tiled=True)
-    packed = call(state_kernel, shape((heads * PAD, PAD), F32), [SMEM, VMEM, VMEM], "own_state")(live, k, v)
-    state = sums_beyond(packed, z, 1)
-    w, num = call(
-        weights_kernel,
-        (shape((heads, n, n), BF), shape((heads * PAD, n), F32)),
-        [VMEM] * 3,
-        "own_weights",
-    )(q, k, v)
-    attn, numer = call(
+    packed = call(state_kernel, shape((heads * PAD, PAD), F32), [SMEM] * 2 + [VMEM] * 2, "own_state")(place, lengths, k, v)
+    num, weighed = call(weights_kernel, (shape((heads * PAD, n), F32), token), [VMEM] * 3, "own_weights")(q, k, v)
+    state = sums_beyond(packed, z, 1, weighed)
+    terms, numer, summed = call(
         attend_kernel,
-        (shape((width, n), BF), shape((heads * PAD, n), F32)),
-        [SMEM] + [VMEM] * 3,
+        (shape((proj.shape[1], n), BF), shape((heads * PAD, n), F32), token),
+        [SMEM] * 2 + [VMEM] * 4,
         "attend",
-    )(live, q, num, state)
-    terms = lax.dot_general(proj, attn, (((0,), (0,)), ((), ())), preferred_element_type=F32).astype(BF)
+    )(place, lengths, q, num, state, proj)
     mixed = lax.psum_scatter(terms, "y", scatter_dimension=0, tiled=True)
     dn, adj = call(
         adjoint_kernel,
         (shape((heads * PAD, n), BF), shape((heads * PAD, PAD), F32)),
-        [SMEM] + [VMEM] * 4 + [ANY],
+        [SMEM] * 2 + [VMEM] * 5,
         "own_adjoint",
-    )(live, cot_all, proj, q, numer, terms)
-    adj_next = sums_beyond(adj, z, -1)
-    gq, gk, gv = call(
+    )(place, lengths, cot_all, proj, q, numer, summed)
+    gq, gk, gv, gradients = call(
         local_grad_kernel,
-        (shape((width, n), BF), shape((width, n), F32), shape((width, n), F32)),
-        [SMEM] + [VMEM] * 6,
+        (shape((width, n), BF), shape((width, n), F32), shape((width, n), F32), token),
+        [SMEM] * 2 + [VMEM] * 5,
         "own_gradients",
-    )(live, q, k, v, w, dn, state)
+    )(place, lengths, q, k, v, dn, state)
+    adj_next = sums_beyond(adj, z, -1, gradients)
     gk, gv = call(
         far_grad_kernel,
         (shape((width, n), BF), shape((width, n), BF)),
-        [SMEM] + [VMEM] * 5,
+        [SMEM] * 2 + [VMEM] * 5,
         "far_gradients",
-    )(live, k, v, gk, gv, adj_next)
+    )(place, lengths, k, v, gk, gv, adj_next)
     return mixed, gq.T, gk.T, gv.T
 
 

time: 123 us -> 122 us (level)
  the two profiles are of different devices: /device:TPU:4 before, /device:TPU:2 now
where the time goes in v3:
time: 122 us; the launch traced here: 121 us
  blocking collectives  57.7 us (47%)
  starting transfers between devices  17.7 us (15%)
  between operations  14.1 us (12%)
  waiting for transfers between devices  12.1 us (10%)
  Pallas kernels  11.8 us (10%)
  local copies, waits for them, and re-layouts  7.95 us (7%)
    all_to_all x2, blocking collectives, sums_beyond(): everyone = lax.all_to_all(totals, 'z', 0, 0)  40.5 us
    all_to_all x2, starting transfers between devices, sums_beyond(): mine = lax.all_to_all(packed.reshape(8, rows, PAD), PLANE, 0, 0)  17.6 us
    all_to_all x2, blocking collectives, sums_beyond(): return lax.all_to_all(back, PLANE, 0, 0).reshape(8 * rows, PAD)  17.2 us
    unnamed x26, local copies, waits for them, and re-layouts  7.95 us
    reduce_scatter x1, waiting for transfers between devices, per_device(): mixed = lax.psum_scatter(terms, 'y', scatter_dimension=0, tiled=True)  5.19 us
    all_gather x1, waiting for transfers between devices, per_device(): cot_all = lax.all_gather(cot, 'y', axis=0, tiled=True)  3.14 us
    all_to_all x2, waiting for transfers between devices, sums_beyond(): mine = lax.all_to_all(packed.reshape(8, rows, PAD), PLANE, 0, 0)  3.11 us
    pallas_call x1, Pallas kernels, per_device(): call(attend_kernel, (shape((proj.shape[1], n), BF), shape((heads * PAD, n...  2.99 us
  transfers between devices with their start and end apart: 4, of which 4 were waited for; matrix products, arithmetic and copies ran while one was open for 0% of the time, Pallas kernels for 10%

profile of v3, /device:TPU:2, one launch (start us, length us, event | category | flops | bytes accessed | tf_op | source)
XLA Modules:
  0.0 121.4 jit_solution(14521359279590436062)
XLA Ops:
  7.2 0.7 all-gather.2.cloned.1.call-update
  7.9 0.9 copy-done.1
  8.9 0.9 copy-done.4
  10.5 1.4 %own_state.1 = f32[256,128]{1,0:T(8,128)} custom-call(s32[1]{0:T(128)} %bitcast.place_ref, s32[96]{0:T(128)S(1)} %copy-done.11, bf16[224,512]{1,0:T(8,128)(2,1)S(1)} %bitcast.12, bf16[224,512]{1,0:T(8,128)(2,1)S(1)} %bitcast.16), custom_call_target="tpu_custom_call" | custom-call | flops 1000000 | bytes 1000000 | tf_op jit(solution)/shard_map/own_state/pallas_call | solution.py:227
  11.9 12.8 %all-to-all-start = ((f32[8,32,128]{2,1,0:T(8,128)}), f32[8,32,128]{2,1,0:T(8,128)S(1)}, u32[]{:S(2)}, u32[]{:S(2)}) async-start(f32[8,32,128]{2,1,0:T(8,128)} %bitcast.5), calls=%async_computation | async-start | bytes 262144 | tf_op jit(solution)/shard_map/all_to_all | solution.py:103
  24.7 0.9 copy-done.2
  25.7 0.9 copy-done.5
  26.6 0.9 copy-done.7
  27.5 0.9 own_weights.1
  28.4 1.0 all-to-all-done.mine_ref.refs_1_
  29.4 18.7 %all_to_all.30.refs_2_ = bf16[12,32,128]{2,1,0:T(8,128)(2,1)S(1)} all-to-all(bf16[12,32,128]{2,1,0:T(8,128)(2,1)S(1)} %plane_total.2), channel_id=1, replica_groups=mesh['z'=12,'x'=4,'c'=2,'y'=8] {'z'}, dimensions={0} | all-to-all | bytes 196608 | tf_op jit(solution)/shard_map/all_to_all | solution.py:105
  48.2 8.7 %all_to_all.31 = f32[8,32,128]{2,1,0:T(8,128)S(1)} all-to-all(f32[8,32,128]{2,1,0:T(8,128)S(1)} %spread.2), channel_id=1, replica_groups=mesh['z'=12,'x'=4,'c'=2,'y'=8] {'x','c'}, dimensions={0} | all-to-all | bytes 262144 | tf_op jit(solution)/shard_map/all_to_all | solution.py:109
  56.9 0.9 copy-done.8
  57.8 3.0 %attend.1 = (bf16[2240,512]{1,0:T(8,128)(2,1)}, f32[256,512]{1,0:T(8,128)S(1)}, f32[8,128]{1,0:T(8,128)S(1)}) custom-call(s32[1]{0:T(128)} %bitcast.place_ref, s32[96]{0:T(128)S(1)} %copy-done.12, bf16[224,512]{1,0:T(8,128)(2,1)S(1)} %bitcast.21, f32[256,512]{1,0:T(8,128)S(1)} %get-tuple-element.17.num_ref, f32[256,128]{1,0:T(8,128)S(1)} %bitcast.24, ...), custom_call_target="tpu_custom_call" | custom-call | flops 1000000 | bytes 1000000 | tf_op jit(solution)/shard_map/attend/pallas_call | solution.py:230
  60.9 3.1 %all-gather.2.cloned.1.call-done.cot_ref = bf16[2240,512]{1,0:T(8,128)(2,1)} async-done(((bf16[280,512]{1,0:T(8,128)(2,1)}), bf16[2240,512]{1,0:T(8,128)(2,1)}) %all-gather.2.cloned.1.call-update) | async-done | bytes 2293776 | tf_op jit(solution)/shard_map/all_gather | solution.py:226
  64.0 1.6 %copy-done.10 = bf16[2240,512]{1,0:T(8,128)(2,1)S(1)} copy-done((bf16[2240,512]{1,0:T(8,128)(2,1)S(1)}, bf16[2240,512]{1,0:T(8,128)(2,1)}, u32[]{:S(2)}) %copy-start.10) | copy-done | bytes 2293784
  65.7 2.1 %own_adjoint.1 = (bf16[256,512]{1,0:T(8,128)(2,1)S(1)}, f32[256,128]{1,0:T(8,128)}) custom-call(s32[1]{0:T(128)} %bitcast.place_ref, s32[96]{0:T(128)S(1)} %copy-done.12, bf16[2240,512]{1,0:T(8,128)(2,1)S(1)} %copy-done.10, bf16[224,2240]{1,0:T(8,128)(2,1)S(1)} %copy-done, bf16[224,512]{1,0:T(8,128)(2,1)S(1)} %bitcast.22, ...), custom_call_target="tpu_custom_call" | custom-call | flops 1000000 | bytes 1000000 | tf_op jit(solution)/shard_map/own_adjoint/pallas_call | solution.py:237
  67.8 4.8 %all-to-all-start.3 = ((f32[8,32,128]{2,1,0:T(8,128)}), f32[8,32,128]{2,1,0:T(8,128)S(1)}, u32[]{:S(2)}, u32[]{:S(2)}) async-start(f32[8,32,128]{2,1,0:T(8,128)} %bitcast.8), calls=%async_computation.4 | async-start | bytes 262144 | tf_op jit(solution)/shard_map/all_to_all | solution.py:103
  72.6 2.5 %own_gradients.1 = (bf16[224,512]{1,0:T(8,128)(2,1)}, f32[224,512]{1,0:T(8,128)S(1)}, f32[224,512]{1,0:T(8,128)S(1)}, f32[8,128]{1,0:T(8,128)S(1)}) custom-call(s32[1]{0:T(128)} %bitcast.place_ref, s32[96]{0:T(128)S(1)} %copy-done.12, bf16[224,512]{1,0:T(8,128)(2,1)S(1)} %bitcast.23, bf16[224,512]{1,0:T(8,128)(2,1)S(1)} %bitcast.14, ...), custom_call_target="tpu_custom_call" | custom-call | flops 1000000 | bytes 1000000 | tf_op jit(solution)/shard_map/own_gradients/pallas_call | solution.py:243
  75.2 2.1 %all-to-all-done.3.mine_ref.refs_1_ = f32[8,32,128]{2,1,0:T(8,128)S(1)} async-done(((f32[8,32,128]{2,1,0:T(8,128)}), f32[8,32,128]{2,1,0:T(8,128)S(1)}, u32[]{:S(2)}, u32[]{:S(2)}) %all-to-all-start.3) | async-done | bytes 131104 | tf_op jit(solution)/shard_map/all_to_all | solution.py:103
  77.3 21.8 %all_to_all.32.refs_2_ = bf16[12,32,128]{2,1,0:T(8,128)(2,1)S(1)} all-to-all(bf16[12,32,128]{2,1,0:T(8,128)(2,1)S(1)} %plane_total.3), channel_id=1, replica_groups=mesh['z'=12,'x'=4,'c'=2,'y'=8] {'z'}, dimensions={0} | all-to-all | bytes 196608 | tf_op jit(solution)/shard_map/all_to_all | solution.py:105
  99.1 8.5 %all_to_all.33 = f32[8,32,128]{2,1,0:T(8,128)S(1)} all-to-all(f32[8,32,128]{2,1,0:T(8,128)S(1)} %spread.3), channel_id=1, replica_groups=mesh['z'=12,'x'=4,'c'=2,'y'=8] {'x','c'}, dimensions={0} | all-to-all | bytes 262144 | tf_op jit(solution)/shard_map/all_to_all | solution.py:109
  107.6 1.7 %far_gradients.1 = (bf16[224,512]{1,0:T(8,128)(2,1)}, bf16[224,512]{1,0:T(8,128)(2,1)}) custom-call(s32[1]{0:T(128)} %bitcast.place_ref, s32[96]{0:T(128)S(1)} %copy-done.12, bf16[224,512]{1,0:T(8,128)(2,1)S(1)} %bitcast.15, bf16[224,512]{1,0:T(8,128)(2,1)S(1)} %bitcast.19, f32[224,512]{1,0:T(8,128)S(1)} %get-tuple-element.24.gk_ref, ...), custom_call_target="tpu_custom_call" | custom-call | flops 1000000 | bytes 1000000 | tf_op jit(solution)/shard_map/far_gradients/pallas_call | solution.py:250
  109.3 5.2 %reduce-scatter.2.cloned.1.call-done = bf16[280,512]{1,0:T(8,128)(2,1)} async-done(((bf16[2240,512]{1,0:T(8,128)(2,1)}), bf16[280,512]{1,0:T(8,128)(2,1)}) %reduce-scatter.2.cloned.1.call-update) | async-done | bytes 286736 | tf_op jit(solution)/shard_map/reduce_scatter | solution.py:236
  (26 shorter events, 0.9 us)
Async XLA Ops:
  7.2 49.7 %copy-start = (bf16[224,2240]{1,0:T(8,128)(2,1)S(1)}, bf16[224,2240]{1,0:T(8,128)(2,1)}, u32[]{:S(2)}) copy-start(bf16[224,2240]{1,0:T(8,128)(2,1)} %proj_ref.3) | copy-start | bytes 3010564
  7.2 56.8 %all-gather.2.cloned.1.call-start = ((), (), s32[]{:S(2)}) async-start(), calls=%async_computation.8 | async-start | bytes 2580480 | tf_op jit(solution)/shard_map/all_gather | solution.py:226
  7.9 0.9 copy-start.1
  8.9 0.9 copy-start.4
  9.8 0.7 copy-start.11
  10.5 46.4 %copy-start.12 = (s32[96]{0:T(128)S(1)}, s32[96]{0:T(128)}, u32[]{:S(2)}) copy-start(s32[96]{0:T(128)} %lengths_ref.9) | copy-start | bytes 1156
  11.9 17.5 %all-to-all-start = ((f32[8,32,128]{2,1,0:T(8,128)}), f32[8,32,128]{2,1,0:T(8,128)S(1)}, u32[]{:S(2)}, u32[]{:S(2)}) async-start(f32[8,32,128]{2,1,0:T(8,128)} %bitcast.5), calls=%async_computation | async-start | bytes 262144 | tf_op jit(solution)/shard_map/all_to_all | solution.py:103
  24.7 89.8 %reduce-scatter.2.cloned.1.call-start = ((), (), s32[]{:S(2)}) async-start(), calls=%async_computation.7 | async-start | bytes 2580480 | tf_op jit(solution)/shard_map/reduce_scatter | solution.py:236
  24.7 0.9 copy-start.2
  25.6 0.9 copy-start.5
  26.6 0.9 copy-start.7
  48.2 15.8 %copy-start.9 = (bf16[512,224]{0,1:T(8,128)(2,1)S(1)}, bf16[512,224]{0,1:T(8,128)(2,1)}, u32[]{:S(2)}) copy-start(bf16[512,224]{0,1:T(8,128)(2,1)} %param.6) | copy-start | bytes 688132
  56.9 0.9 copy-start.8
  60.9 11.8 %copy-start.3 = (bf16[512,224]{0,1:T(8,128)(2,1)S(1)}, bf16[512,224]{0,1:T(8,128)(2,1)}, u32[]{:S(2)}) copy-start(bf16[512,224]{0,1:T(8,128)(2,1)} %param.7) | copy-start | bytes 688132
  60.9 11.8 %copy-start.6 = (bf16[512,224]{0,1:T(8,128)(2,1)S(1)}, bf16[512,224]{0,1:T(8,128)(2,1)}, u32[]{:S(2)}) copy-start(bf16[512,224]{0,1:T(8,128)(2,1)} %param.8) | copy-start | bytes 688132
  64.0 1.6 %copy-start.10 = (bf16[2240,512]{1,0:T(8,128)(2,1)S(1)}, bf16[2240,512]{1,0:T(8,128)(2,1)}, u32[]{:S(2)}) copy-start(bf16[2240,512]{1,0:T(8,128)(2,1)} %all-gather.2.cloned.1.call-done.cot_ref) | copy-start | bytes 6881284
  67.8 9.5 %all-to-all-start.3 = ((f32[8,32,128]{2,1,0:T(8,128)}), f32[8,32,128]{2,1,0:T(8,128)S(1)}, u32[]{:S(2)}, u32[]{:S(2)}) async-start(f32[8,32,128]{2,1,0:T(8,128)} %bitcast.8), calls=%async_computation.4 | async-start | bytes 262144 | tf_op jit(solution)/shard_map/all_to_all | solution.py:103
Sparse Core Ops, SparseCore 0:
  10.4 53.5 all-gather.1
  67.7 46.7 reduce-scatter.1
